TPU v7x, 128 devices: a whole 4x4x4 slice. The times are simulated.
128 devices in a mesh: rows: 16 (over y, z), cols: 4 (over x_lo, core), dp: 2 (over x_hi).
Axes of the slice: x: 4 (x_hi: 2, x_lo: 2; x = x_hi * 2 + x_lo), y: 4, z: 4, core: 2. Of those that a mesh axis runs over, the one named last changes fastest.
Arguments:
- panel_weight: float32 [8192, 1024], P('rows', 'cols'), may hold values from -6 to 6
- rest_weight: float32 [8192, 15360], P('rows', 'cols'), may hold values from -6 to 6
- hinv_diag: float32 [1024, 1024], P('rows'), as said below
- hinv_off: float32 [1024, 15360], P('rows', 'cols'), may hold values from -0.1875 to 0.1875
- calib_panel: bfloat16 [1024, 1024], P('dp', 'cols'), may hold values from -0.125 to 0.125
- calib_rest: bfloat16 [1024, 15360], P('dp', 'cols'), may hold values from -0.125 to 0.125
- prune_blocks: int32 [128, 8], P('rows'), may hold values from 0 to 15, as said below
Outputs:
- pruned_panel: float32 [8192, 1024], P('rows', 'cols')
- pruned_rest: float32 [8192, 15360], P('rows', 'cols')
- layer_out: bfloat16 [1024, 8192], P('dp', ('rows', 'cols'))
- recon_error: float32 [1024, 8192], P('dp', ('rows', 'cols'))
Inputs may be any that keep to these rules, and one draw needn't show every extreme that they name: `prune_blocks`: each row names 8 different column blocks of the panel's 16. `hinv_diag`: upper triangular with a positive diagonal.
All inputs are finite; a program needn't handle non-finite values.
Results may differ from a plain program's by a relative error of at most 0.0098.
Values sent between devices are 32-bit elements; how exact they have to be, the bound alone decides.
No kernel may reach another device: no remote copies, remote signals or barrier semaphores. Data moves between devices by JAX's collectives and lax.ppermute only.
A program may use at most 128 MiB of HBM per device.

v0:
```python
import jax
import jax.numpy as jnp
from jax import lax
from jax.sharding import PartitionSpec as P

BLOCK = 64


def from_root(value, axis, source):
    kept = jnp.where(lax.axis_index(axis) == source, value, 0).astype(value.dtype)
    return lax.psum(kept, axis)


def block_mask(prune_blocks, panel):
    count = panel // BLOCK
    hits = prune_blocks[:, :, None] == jnp.arange(count, dtype=jnp.int32)[None, None, :]
    dense = jnp.sum(hits.astype(jnp.float32), axis=1)
    return jnp.repeat(jnp.repeat(dense, BLOCK, axis=0), BLOCK, axis=1)


def project(inputs, weights):
    return jnp.einsum("tk,rk->tr", inputs, weights, preferred_element_type=jnp.float32)


def upper_inverse(square):
    side = square.shape[0]
    diagonal = jnp.diagonal(square)
    identity = jnp.eye(side, dtype=jnp.float32)
    power = -(jnp.triu(square, 1) / diagonal[:, None])
    result = identity + power
    for level in range(max(side.bit_length() - 2, 0)):
        power = jnp.dot(power, power, precision=lax.Precision.HIGHEST)
        result = jnp.dot(result, identity + power, precision=lax.Precision.HIGHEST)
    return result / diagonal[None, :]


def solve_block(target, square):
    return jnp.dot(target, upper_inverse(square), precision=lax.Precision.HIGHEST)


def local_errors(work, mask, square):
    pieces = []
    for block in range(work.shape[1] // BLOCK):
        lower_edge = block * BLOCK
        upper_edge = lower_edge + BLOCK
        target = work[:, lower_edge:upper_edge] * mask[:, lower_edge:upper_edge]
        err = solve_block(target, square[lower_edge:upper_edge, lower_edge:upper_edge])
        work = work - jnp.dot(
            err, square[lower_edge:upper_edge, :], precision=lax.Precision.HIGHEST
        )
        pieces.append(err)
    return jnp.concatenate(pieces, axis=1)


def on_device(
    panel_weight, rest_weight, hinv_diag, hinv_off, calib_panel, calib_rest, prune_blocks
):
    col_count = lax.axis_size("cols")
    col_index = lax.axis_index("cols")
    own = panel_weight.shape[1]
    panel = own * col_count
    mask_full = block_mask(prune_blocks, panel)
    mask_own = lax.dynamic_slice_in_dim(mask_full, col_index * own, own, 1)
    upper = lax.all_gather(hinv_diag, "rows", axis=0, tiled=True)
    upper_own = lax.dynamic_slice_in_dim(upper, col_index * own, own, 1)
    square = lax.dynamic_slice_in_dim(upper_own, col_index * own, own, 0)
    work = panel_weight
    pieces = []
    for step in range(col_count):
        mine = local_errors(work, mask_own, square)
        sent = from_root(mine, "cols", step)
        work = work - jnp.dot(
            sent, upper_own[step * own : (step + 1) * own, :], precision=lax.Precision.HIGHEST
        )
        pieces.append(sent)
    errors = jnp.concatenate(pieces, axis=1)
    kept_panel = work * (1.0 - mask_own)
    new_rest = rest_weight - jnp.dot(
        errors,
        lax.all_gather(hinv_off, "rows", axis=0, tiled=True),
        precision=lax.Precision.HIGHEST,
    )
    pruned_sum = project(calib_panel, kept_panel.astype(jnp.bfloat16)) + project(
        calib_rest, new_rest.astype(jnp.bfloat16)
    )
    dense_sum = project(calib_panel, panel_weight.astype(jnp.bfloat16)) + project(
        calib_rest, rest_weight.astype(jnp.bfloat16)
    )
    pruned_out, dense_out = (
        lax.psum_scatter(pruned_sum, "cols", scatter_dimension=1, tiled=True),
        lax.psum_scatter(dense_sum, "cols", scatter_dimension=1, tiled=True),
    )
    return (kept_panel, new_rest, pruned_out.astype(jnp.bfloat16), pruned_out - dense_out)


def solution(mesh):
    in_specs = (
        P("rows", "cols"),
        P("rows", "cols"),
        P("rows", None),
        P("rows", "cols"),
        P("dp", "cols"),
        P("dp", "cols"),
        P("rows", None),
    )
    out_specs = (
        P("rows", "cols"),
        P("rows", "cols"),
        P("dp", ("rows", "cols")),
        P("dp", ("rows", "cols")),
    )
    return jax.shard_map(
        on_device, mesh=mesh, in_specs=in_specs, out_specs=out_specs, check_vma=False
    )
```

profile of v0, /device:TPU:1, one launch (start us, length us, event | category | flops | bytes accessed | tf_op | source)
XLA Modules:
  0.0 437.9 jit_solution(8448390797991927327)
XLA Ops:
  10.2 54.8 %all-gather.3.cloned.1.call-done = f32[1024,1024]{1,0:T(8,128)} async-done(((f32[64,1024]{1,0:T(8,128)}), f32[1024,1024]{1,0:T(8,128)}) %all-gather.3.cloned.1.call-update) | async-done | bytes 4194320 | tf_op jit(solution)/shard_map/all_gather | solution.py:64
  77.4 1.6 convolution_subtract_fusion.8
  79.3 1.6 convolution_subtract_fusion.7
  81.3 1.6 fusion.73
  84.1 37.7 %all-reduce.5.cloned.1.call-done = f32[512,256]{0,1:T(8,128)} async-done(((f32[512,256]{0,1:T(8,128)}), f32[512,256]{0,1:T(8,128)}) %all-reduce.5.cloned.1.call-update) | async-done | bytes 524304 | tf_op jit(solution)/shard_map/psum | solution.py:11
  121.8 1.8 convolution_subtract_fusion.12
  126.3 1.6 convolution_subtract_fusion.5
  128.3 1.6 fusion.71
  131.3 38.5 %all-reduce.7.cloned.1.call-done = f32[512,256]{0,1:T(8,128)} async-done(((f32[512,256]{0,1:T(8,128)}), f32[512,256]{0,1:T(8,128)}) %all-reduce.7.cloned.1.call-update) | async-done | bytes 524304 | tf_op jit(solution)/shard_map/psum | solution.py:11
  169.7 1.8 convolution_subtract_fusion.11
  171.8 1.6 convolution_subtract_fusion.4
  173.8 1.6 convolution_subtract_fusion.3
  175.7 1.6 fusion.69
  178.6 38.6 %all-reduce.9.cloned.1.call-done = f32[512,256]{0,1:T(8,128)} async-done(((f32[512,256]{0,1:T(8,128)}), f32[512,256]{0,1:T(8,128)}) %all-reduce.9.cloned.1.call-update) | async-done | bytes 524304 | tf_op jit(solution)/shard_map/psum | solution.py:11
  217.2 1.8 convolution_subtract_fusion.10
  219.3 1.6 convolution_subtract_fusion.2
  221.2 1.6 convolution_subtract_fusion.1
  226.6 6.7 %fusion = f32[512,512]{0,1:T(8,128)S(1)} fusion(bf16[512,3840]{1,0:T(8,128)(2,1)} %param.12, f32[512,3840]{1,0:T(8,128)} %param.8), kind=kOutput, calls=%fused_computation.5 | convolution fusion | flops 2015232000 | bytes 12845056 | tf_op jit(solution)/shard_map/tk,rk->tr/dot_general | solution.py:22
  234.9 29.7 %all-reduce.11.cloned.1.call-done = f32[512,256]{0,1:T(8,128)} async-done(((f32[512,256]{0,1:T(8,128)}), f32[512,256]{0,1:T(8,128)}) %all-reduce.11.cloned.1.call-update) | async-done | bytes 524304 | tf_op jit(solution)/shard_map/psum | solution.py:11
  264.7 1.8 fusion.12
  266.5 106.8 %all-gather.5.cloned.1.call-done = f32[1024,3840]{1,0:T(8,128)} async-done(((f32[64,3840]{1,0:T(8,128)}), f32[1024,3840]{1,0:T(8,128)}) %all-gather.5.cloned.1.call-update) | async-done | bytes 15728656 | tf_op jit(solution)/shard_map/all_gather | solution.py:80
  373.3 30.2 %convolution_subtract_fusion = f32[512,3840]{1,0:T(8,128)S(1)} fusion(f32[512,3840]{1,0:T(8,128)} %param.8, f32[1024,3840]{1,0:T(8,128)} %all-gather.5.cloned.1.call-done, f32[512,256]{0,1:T(8,128)} %all-reduce.11.cloned.1.call-done, f32[512,256]{0,1:T(8,128)} %all-reduce.9.cloned.1.call-done, f32[512,256]{0,1:T(8,128)} %all-reduce.7.cloned.1.call-done, ...), kind=kOutput, calls=%fused_computation.4 | convolution fusion | flops 24162729984 | bytes 33554432 | tf_op jit(solution)/shard_map/dot_general | solution.py:78
  403.5 2.2 fusion.2
  409.1 19.3 %reduce-scatter.3.cloned.1.call-done = f32[512,128]{0,1:T(8,128)} async-done(((f32[512,512]{0,1:T(8,128)}), f32[512,128]{0,1:T(8,128)}) %reduce-scatter.3.cloned.1.call-update) | async-done | bytes 262160 | tf_op jit(solution)/shard_map/reduce_scatter | solution.py:90
  (109 shorter events, 35.5 us)
Async XLA Ops:
  7.2 226.1 %copy-start = (bf16[512,256]{1,0:T(8,128)(2,1)S(1)}, bf16[512,256]{1,0:T(8,128)(2,1)}, u32[]{:S(2)}) copy-start(bf16[512,256]{1,0:T(8,128)(2,1)} %param.11) | copy-start | bytes 786436
  7.2 57.9 %all-gather.3.cloned.1.call-start = ((), (), s32[]{:S(2)}) async-start(), calls=%async_computation.2 | async-start | bytes 4456448 | tf_op jit(solution)/shard_map/all_gather | solution.py:64
  7.9 113.9 %all-reduce.5.cloned.1.call-start = ((), (), s32[]{:S(2)}) async-start(), calls=%async_computation.3 | async-start | bytes 1048576 | tf_op jit(solution)/shard_map/psum | solution.py:11
  84.1 85.7 %all-reduce.7.cloned.1.call-start = ((), (), s32[]{:S(2)}) async-start(), calls=%async_computation.4 | async-start | bytes 1048576 | tf_op jit(solution)/shard_map/psum | solution.py:11
  123.6 0.8 copy-start.2
  126.0 43.8 %copy-start.3 = (f32[512,256]{0,1:T(8,128)S(1)}, f32[512,256]{0,1:T(8,128)}, u32[]{:S(2)}) copy-start(f32[512,256]{0,1:T(8,128)} %copy-done.2) | copy-start | bytes 1572868
  131.1 86.2 %all-reduce.9.cloned.1.call-start = ((), (), s32[]{:S(2)}) async-start(), calls=%async_computation.5 | async-start | bytes 1048576 | tf_op jit(solution)/shard_map/psum | solution.py:11
  178.5 86.2 %all-reduce.11.cloned.1.call-start = ((), (), s32[]{:S(2)}) async-start(), calls=%async_computation.6 | async-start | bytes 1048576 | tf_op jit(solution)/shard_map/psum | solution.py:11
  226.0 147.4 %all-gather.5.cloned.1.call-start = ((), (), s32[]{:S(2)}) async-start(), calls=%async_computation.7 | async-start | bytes 16711680 | tf_op jit(solution)/shard_map/all_gather | solution.py:80
  226.5 6.8 %copy-start.4 = (f32[512,256]{1,0:T(8,128)S(1)}, f32[512,256]{1,0:T(8,128)}, u32[]{:S(2)}) copy-start(f32[512,256]{1,0:T(8,128)} %param.7) | copy-start | bytes 1572868
  226.6 182.5 %reduce-scatter.5.cloned.1.call-start = ((), (), s32[]{:S(2)}) async-start(), calls=%async_computation.9 | async-start | bytes 1310720 | tf_op jit(solution)/shard_map/reduce_scatter | solution.py:91
  234.7 193.7 %reduce-scatter.3.cloned.1.call-start = ((), (), s32[]{:S(2)}) async-start(), calls=%async_computation.8 | async-start | bytes 1310720 | tf_op jit(solution)/shard_map/reduce_scatter | solution.py:90
  373.3 30.2 %copy-start.5 = (bf16[512,3840]{1,0:T(8,128)(2,1)S(1)}, bf16[512,3840]{1,0:T(8,128)(2,1)}, u32[]{:S(2)}) copy-start(bf16[512,3840]{1,0:T(8,128)(2,1)} %param.12) | copy-start | bytes 11796484
  403.5 3.2 copy-start.1
Sparse Core Ops, SparseCore 0:
  10.2 54.8 all-gather.2
  84.2 37.5 all-reduce.4
  131.2 38.5 all-reduce.6
  178.6 38.5 all-reduce.8
  226.1 38.5 all-reduce.10
  266.7 106.5 all-gather.4
  375.7 20.2 reduce-scatter.4
  408.2 20.0 reduce-scatter.2
where the time goes:
time: 439 us; the launch traced here: 438 us
  waiting for transfers between devices  327 us (74%)
  matrix products  80.2 us (18%)
  between operations  14.9 us (3%)
  local copies, waits for them, and re-layouts  10.1 us (2%)
  other arithmetic  5.27 us (1%)
    psum x4, waiting for transfers between devices, from_root(): return lax.psum(kept, axis)  145 us
    all_gather x1, waiting for transfers between devices, on_device(): lax.all_gather(hinv_off, 'rows', axis=0, tiled=True)  107 us
    all_gather x1, waiting for transfers between devices, on_device(): upper = lax.all_gather(hinv_diag, 'rows', axis=0, tiled=True)  54.8 us
    dot_general x1, matrix products, on_device(): jnp.dot(errors, lax.all_gather(hinv_off, 'rows', axis=0, tiled=True), pre...  30.2 us
    reduce_scatter x1, waiting for transfers between devices, on_device(): lax.psum_scatter(pruned_sum, 'cols', scatter_dimension=1, tiled=True)  19.3 us
    dot_general x12, matrix products, local_errors(): jnp.dot(err, square[lower_edge:upper_edge, :], precision=lax.Precision.HI...  19.2 us
    dot_general x4, matrix products, project(): jnp.einsum('tk,rk->tr', inputs, weights, preferred_element_type=jnp.float32)  11.6 us
  transfers between devices with their start and end apart: 8, of which 7 were waited for; matrix products, arithmetic and copies ran while one was open for 11% of the time, Pallas kernels for 0%

commit v1 on v0

v1 whole, which is shorter than its diff:
```python
import functools

import jax
import jax.numpy as jnp
from jax import lax
from jax.experimental import pallas as pl
from jax.experimental.pallas import tpu as pltpu
from jax.sharding import PartitionSpec as P

BLOCK = 64
RING = 4
OFFSETS = (0, -1, 1, 2)
F32 = jnp.float32
BF16 = jnp.bfloat16
HIGHEST = lax.Precision.HIGHEST


def split(value):
    high = value.astype(BF16)
    low = (value - high.astype(F32)).astype(BF16)
    return high, low


def dot(left, right):
    return jnp.dot(left, right, preferred_element_type=F32)


def dot3(left, right):
    return dot(left[0], right[0]) + dot(left[1], right[0]) + dot(left[0], right[1])


def dot_nt(left, right):
    return lax.dot_general(left, right, (((1,), (1,)), ((), ())), preferred_element_type=F32)


def along(value, axis, step):
    def shift(y, z):
        if axis == "y":
            return ((y + step) % RING) * RING + z
        return y * RING + (z + step) % RING

    pairs = [(y * RING + z, shift(y, z)) for y in range(RING) for z in range(RING)]
    return lax.ppermute(value, "rows", pairs)


def swap(value, bit):
    return lax.ppermute(value, "cols", [(i, i ^ bit) for i in range(4)])


def ring_gather(value, axis):
    half = value.shape[0] // 2
    before, after = along(value, axis, 1), along(value, axis, -1)
    far_top, far_bottom = along(before[:half], axis, 1), along(after[half:], axis, -1)
    return jnp.concatenate([value, before, after, far_top, far_bottom], axis=0)


def factor_kernel(place, diag_ref, rows_ref, out_ref):
    block, core = place[0], place[1]
    side = BLOCK
    row = lax.broadcasted_iota(jnp.int32, (side, side), 0)
    column = lax.broadcasted_iota(jnp.int32, (side, side), 1)
    square = diag_ref[...]
    identity = (row == column).astype(F32)
    down = jnp.sum(square * identity, axis=1, keepdims=True)
    across = jnp.sum(square * identity, axis=0, keepdims=True)
    power = jnp.where(column > row, -(square / down), 0.0)
    inverse = identity + power
    for _ in range(side.bit_length() - 2):
        power = jnp.dot(power, power, precision=HIGHEST, preferred_element_type=F32)
        inverse = jnp.dot(inverse, identity + power, precision=HIGHEST, preferred_element_type=F32)
    inverse = inverse / across
    width = out_ref.shape[1]
    start = pl.multiple_of(core * width, width)
    mine = rows_ref[:, pl.ds(start, width)]
    local = lax.broadcasted_iota(jnp.int32, (side, width), 1) + start - block * side
    wide_row = lax.broadcasted_iota(jnp.int32, (side, width), 0)
    inside = (local >= 0) & (local < side)
    mine = jnp.where(inside, (local == wide_row).astype(F32), mine)
    out_ref[...] = jnp.dot(inverse, mine, precision=HIGHEST, preferred_element_type=F32)


def chain_kernel(
    place, prune_ref, w0, w1, w2, w3, near_ref, far_ref,
    high_ref, low_ref, kept_ref,
    work, fac_high, fac_low, kept,
):
    col, core, y, z = place[2], place[1], place[3], place[4]
    rows, own = w0.shape
    for slot, piece in enumerate((w0, w1, w2, w3)):
        work[col ^ slot] = piece[...]
    half = near_ref.shape[1]
    for which, ref in enumerate((near_ref, far_ref)):
        start = pl.multiple_of((core ^ which) * half, half)
        for zi, zo in enumerate(OFFSETS):
            for yi, yo in enumerate(OFFSETS):
                block = ((y + yo) & 3) * RING + ((z + zo) & 3)
                at = (zi * RING + yi) * BLOCK
                top = pl.multiple_of(block * BLOCK, BLOCK)
                high, low = split(ref[at : at + BLOCK, :])
                fac_high[pl.ds(top, BLOCK), pl.ds(start, half)] = high
                fac_low[pl.ds(top, BLOCK), pl.ds(start, half)] = low
    groups = rows // BLOCK
    bits = []
    for group in range(groups):
        word = jnp.int32(0)
        for entry in range(prune_ref.shape[1]):
            word = word | (jnp.int32(1) << prune_ref[group, entry])
        bits.append(jnp.full((BLOCK, 128), word, jnp.int32))
    lane = lax.broadcasted_iota(jnp.int32, (rows, 128), 1)
    upper = lane >> 6
    bits = lax.shift_right_logical(jnp.concatenate(bits, axis=0), upper)
    lower = 1 - upper
    panels = work.shape[0]
    parts = 2
    size = rows // parts
    for panel in range(panels):
        base = panel * own
        for part in range(parts):
            rs = slice(part * size, (part + 1) * size)
            word, first_half = bits[rs], lower[rs]
            left = work[panel, rs, :128]
            right = work[panel, rs, 128:]
            targets = []
            pair_values = [left, right]
            for pair in range(2):
                value = pair_values[pair]
                first = panel * 4 + pair * 2
                top = base + pair * 128
                hit = lax.shift_right_logical(word, first) & 1
                t0 = jnp.where((hit & first_half) != 0, value, 0.0)
                fac = (
                    fac_high[top : top + 128, top : top + 128],
                    fac_low[top : top + 128, top : top + 128],
                )
                step = dot3(split(t0), fac)
                value = jnp.where(first_half != 0, value, value - step)
                target = jnp.where(hit != 0, value, 0.0)
                keep = jnp.where(hit != 0, 0.0, value)
                kept[panel, rs, pair * 128 : (pair + 1) * 128] = keep
                targets.append(target)
                if pair == 0:
                    fac = (
                        fac_high[top : top + 128, top + 128 : top + 256],
                        fac_low[top : top + 128, top + 128 : top + 256],
                    )
                    pair_values[1] = right - dot3(split(target), fac)
            target = split(jnp.concatenate(targets, axis=1))
            r = lax.broadcasted_iota(jnp.int32, (own, own), 0)
            c = lax.broadcasted_iota(jnp.int32, (own, own), 1)
            same = (r // BLOCK) == (c // BLOCK)
            zero = jnp.zeros((own, own), BF16)
            diagonal = (
                jnp.where(same, fac_high[base : base + own, base : base + own], zero),
                jnp.where(same, fac_low[base : base + own, base : base + own], zero),
            )
            errors = split(dot3(target, diagonal))
            high_ref[rs, base : base + own] = errors[0]
            low_ref[rs, base : base + own] = errors[1]
            for later in range(panel + 1, panels):
                to = later * own
                fac = (
                    fac_high[base : base + own, to : to + own],
                    fac_low[base : base + own, to : to + own],
                )
                work[later, rs, :] = work[later, rs, :] - dot3(target, fac)
    kept_ref[...] = kept[col]


def store_slots(place, total, keep_ref, send_ref):
    col = place[2]
    width = keep_ref.shape[2]
    for slot in range(4):
        ref = send_ref if slot & 1 else keep_ref
        group = col ^ slot
        for source in range(4):

            @pl.when(group == source)
            def _():
                ref[slot >> 1] = total[:, source * width : (source + 1) * width]


def forward_kernel(place, panel_ref, calib_panel_ref, rest_ref, calib_ref, keep_ref, send_ref, total):
    step = pl.program_id(0)

    @pl.when(step == 0)
    def _():
        total[...] = dot_nt(calib_panel_ref[...], panel_ref[...].astype(BF16))

    total[...] += dot_nt(calib_ref[...], rest_ref[...].astype(BF16))

    @pl.when(step == pl.num_programs(0) - 1)
    def _():
        store_slots(place, total, keep_ref, send_ref)


def update_kernel(
    place, panel_ref, calib_panel_ref, high_ref, low_ref, rest_ref, factor_ref, calib_ref,
    new_ref, keep_ref, send_ref, total,
):
    step = pl.program_id(0)

    @pl.when(step == 0)
    def _():
        total[...] = dot_nt(calib_panel_ref[...], panel_ref[...].astype(BF16))

    value = rest_ref[...] - dot3((high_ref[...], low_ref[...]), split(factor_ref[...]))
    new_ref[...] = value
    total[...] += dot_nt(calib_ref[...], value.astype(BF16))

    @pl.when(step == pl.num_programs(0) - 1)
    def _():
        store_slots(place, total, keep_ref, send_ref)


SMEM = pl.BlockSpec(memory_space=pltpu.SMEM)
VMEM = pl.BlockSpec(memory_space=pltpu.VMEM)


def params(mib, **more):
    return pltpu.CompilerParams(vmem_limit_bytes=mib * 2**20, **more)


def cost(flops, moved):
    return pl.CostEstimate(flops=flops, bytes_accessed=moved, transcendentals=0)


def slots(rows, tokens):
    shape = jax.ShapeDtypeStruct((2, tokens, rows // 4), F32)
    spec = pl.BlockSpec((2, tokens, rows // 4), lambda i: (0, 0, 0))
    return [shape, shape], [spec, spec]


def whole(shape):
    return pl.BlockSpec(shape, lambda i: (0,) * len(shape))


def tiles(rows, width):
    return pl.BlockSpec((rows, width), lambda i: (0, i))


def forward(place, panel, calib_panel, rest, calib):
    rows, columns = rest.shape
    tokens = calib.shape[0]
    tile = 384
    shapes, specs = slots(rows, tokens)
    return pl.pallas_call(
        forward_kernel,
        grid=(columns // tile,),
        in_specs=[
            SMEM, whole(panel.shape), whole(calib_panel.shape),
            tiles(rows, tile), tiles(tokens, tile),
        ],
        out_specs=specs,
        out_shape=shapes,
        scratch_shapes=[pltpu.VMEM((tokens, rows), F32)],
        compiler_params=params(32),
        cost_estimate=cost(2 * rows * tokens * columns, rows * columns * 4 + tokens * columns * 2),
    )(place, panel, calib_panel, rest, calib)


def update(place, panel, calib_panel, high, low, rest, factor, calib):
    rows, columns = rest.shape
    tokens = calib.shape[0]
    depth = factor.shape[0]
    tile = 384
    shapes, specs = slots(rows, tokens)
    return pl.pallas_call(
        update_kernel,
        grid=(columns // tile,),
        in_specs=[
            SMEM, whole(panel.shape), whole(calib_panel.shape), whole(high.shape), whole(low.shape),
            tiles(rows, tile), tiles(depth, tile), tiles(tokens, tile),
        ],
        out_specs=[tiles(rows, tile)] + specs,
        out_shape=[jax.ShapeDtypeStruct(rest.shape, F32)] + shapes,
        scratch_shapes=[pltpu.VMEM((tokens, rows), F32)],
        compiler_params=params(40),
        cost_estimate=cost(
            2 * rows * columns * (3 * depth + tokens), columns * 4 * (2 * rows + depth)
        ),
    )(place, panel, calib_panel, high, low, rest, factor, calib)


def scatter_sum(keep, send):
    near = keep + swap(send, 1)
    return near[0] + swap(near[1], 2)


def on_device(
    panel_weight, rest_weight, hinv_diag, hinv_off, calib_panel, calib_rest, prune_blocks
):
    col = lax.axis_index("cols")
    block = lax.axis_index("rows")
    core = col % 2
    place = jnp.stack([block, core, col, block // RING, block % RING]).astype(jnp.int32)
    rows, own = panel_weight.shape
    panel = hinv_diag.shape[1]
    gathered = lax.all_gather(hinv_off, "rows", axis=0, tiled=True)

    square = lax.dynamic_slice(hinv_diag, (0, block * BLOCK), (BLOCK, BLOCK))
    mine = pl.pallas_call(
        factor_kernel,
        in_specs=[SMEM, VMEM, VMEM],
        out_specs=VMEM,
        out_shape=jax.ShapeDtypeStruct((BLOCK, panel // 2), F32),
        cost_estimate=cost(2 * 64 * 64 * 1600 * 6, 2 * 64 * 1024 * 4),
    )(place, square, hinv_diag)
    near = ring_gather(ring_gather(mine, "y"), "z")
    far = swap(near, 1)

    across = swap(panel_weight, 2)
    pieces = [panel_weight, swap(panel_weight, 1), across, swap(across, 1)]

    high, low, kept = pl.pallas_call(
        chain_kernel,
        in_specs=[SMEM, SMEM] + [VMEM] * 6,
        out_specs=[VMEM] * 3,
        out_shape=[
            jax.ShapeDtypeStruct((rows, panel), BF16),
            jax.ShapeDtypeStruct((rows, panel), BF16),
            jax.ShapeDtypeStruct((rows, own), F32),
        ],
        scratch_shapes=[
            pltpu.VMEM((4, rows, own), F32),
            pltpu.VMEM((panel, panel), BF16),
            pltpu.VMEM((panel, panel), BF16),
            pltpu.VMEM((4, rows, own), F32),
        ],
        compiler_params=params(40),
        cost_estimate=cost(2 * rows * panel * panel * 6, rows * panel * 8 + panel * panel * 4),
    )(place, prune_blocks, *pieces, near, far)

    dense = scatter_sum(*forward(place, panel_weight, calib_panel, rest_weight, calib_rest))
    new_rest, keep, send = update(
        place, kept, calib_panel, high, low, rest_weight, gathered, calib_rest
    )
    pruned = scatter_sum(keep, send)
    return kept, new_rest, pruned.astype(BF16), pruned - dense


def solution(mesh):
    in_specs = (
        P("rows", "cols"),
        P("rows", "cols"),
        P("rows", None),
        P("rows", "cols"),
        P("dp", "cols"),
        P("dp", "cols"),
        P("rows", None),
    )
    out_specs = (
        P("rows", "cols"),
        P("rows", "cols"),
        P("dp", ("rows", "cols")),
        P("dp", ("rows", "cols")),
    )
    return jax.shard_map(
        on_device, mesh=mesh, in_specs=in_specs, out_specs=out_specs, check_vma=False
    )
```

time: 439 us -> 184 us (0.42)
  waiting for transfers between devices: 327 us -> 91.2 us
  matrix products: 80.2 us -> 0 us
  Pallas kernels: 0 us -> 44.4 us
  starting transfers between devices: 0.73 us -> 22.5 us
    psum x4 -> x0, waiting for transfers between devices: 145 us -> none  [from_root(): return lax.psum(kept, axis)]
    all_gather x2 -> x1, waiting for transfers between devices: 162 us -> 36.2 us  [on_device(): gathered = lax.all_gather(hinv_off, 'rows', axis=0, tiled=True)]
    dot_general x77 -> x0, matrix products: 80.2 us -> none  [the longest x1 30.2 us: on_device(): jnp.dot(errors, lax.all_gather(hinv_off, 'rows', axis=0, tiled=True), pre...]
    ppermute x0 -> x16, waiting for transfers between devices: none -> 54.3 us  [the longest x8 30.4 us: along(): return lax.ppermute(value, 'rows', pairs)]
    pallas_call x0 -> x4, Pallas kernels: none -> 44.4 us  [the longest x1 25.8 us: update(): pl.pallas_call(update_kernel, grid=(columns // tile,), in_specs=[SMEM, wh...]
    ppermute x0 -> x16, starting transfers between devices: none -> 22.5 us  [the longest x8 13.4 us: along(): return lax.ppermute(value, 'rows', pairs)]
    reduce_scatter x2 -> x0, waiting for transfers between devices: 19.3 us -> none  [the longest x1 19.3 us: on_device(): lax.psum_scatter(pruned_sum, 'cols', scatter_dimension=1, tiled=True)]
  transfers between devices with their start and end apart: 8 -> 17, of which waited for: 7 -> 8; matrix products, arithmetic and copies ran while one was open for 11% -> 2% of each run, Pallas kernels for 0% -> 24%
where the time goes in v1:
time: 184 us
  waiting for transfers between devices  91.2 us (50%)
  Pallas kernels  44.4 us (24%)
  starting transfers between devices  22.5 us (12%)
  between operations  14.3 us (8%)
  local copies, waits for them, and re-layouts  9.75 us (5%)
  other arithmetic  1.99 us (1%)
    all_gather x1, waiting for transfers between devices, on_device(): gathered = lax.all_gather(hinv_off, 'rows', axis=0, tiled=True)  36.2 us
    ppermute x8, waiting for transfers between devices, along(): return lax.ppermute(value, 'rows', pairs)  30.4 us
    pallas_call x1, Pallas kernels, update(): pl.pallas_call(update_kernel, grid=(columns // tile,), in_specs=[SMEM, wh...  25.8 us
    ppermute x8, waiting for transfers between devices, swap(): return lax.ppermute(value, 'cols', [(i, i ^ bit) for i in range(4)])  23.9 us
    ppermute x8, starting transfers between devices, along(): return lax.ppermute(value, 'rows', pairs)  13.4 us
    ppermute x8, starting transfers between devices, swap(): return lax.ppermute(value, 'cols', [(i, i ^ bit) for i in range(4)])  9.13 us
    pallas_call x1, Pallas kernels, on_device(): pl.pallas_call(chain_kernel, in_specs=[SMEM, SMEM] + [VMEM] * 6, out_spec...  8.62 us
    unnamed x23, local copies, waits for them, and re-layouts  7.5 us
  transfers between devices with their start and end apart: 17, of which 8 were waited for; matrix products, arithmetic and copies ran while one was open for 2% of the time, Pallas kernels for 24%

profile of v1, /device:TPU:1, one launch (start us, length us, event | category | flops | bytes accessed | tf_op | source)
XLA Modules:
  0.0 184.1 jit_solution(9548864468604540156)
XLA Ops:
  8.6 1.4 constant_dynamic-slice_fusion.diag_ref
  10.1 3.1 %shard_map.102 = f32[64,512]{1,0:T(8,128)} custom-call(s32[5]{0:T(128)} %stack.23.place, f32[64,64]{1,0:T(8,128)} %constant_dynamic-slice_fusion.diag_ref, f32[64,1024]{1,0:T(8,128)} %rows_ref.1), custom_call_target="tpu_custom_call" | custom-call | flops 78643200 | bytes 524288 | tf_op jit(solution)/shard_map/pallas_call | solution.py:301
  13.1 2.1 %collective-permute-start.3 = (f32[64,512]{1,0:T(8,128)}, f32[64,512]{1,0:T(8,128)S(1)}, u32[]{:S(2)}, u32[]{:S(2)}) collective-permute-start(f32[64,512]{1,0:T(8,128)} %shard_map.102), channel_id=1, source_target_pairs={{0,32},{8,40},{16,48},{24,56},{32,64},{40,72},{48,80},{56,88},{64,... | collective-permute-start | bytes 393224 | tf_op jit(solution)/shard_map/ppermute | solution.py:43
  15.3 1.4 collective-permute-start.4
  17.7 2.3 %collective-permute-done.3 = f32[64,512]{1,0:T(8,128)S(1)} collective-permute-done((f32[64,512]{1,0:T(8,128)}, f32[64,512]{1,0:T(8,128)S(1)}, u32[]{:S(2)}, u32[]{:S(2)}) %collective-permute-start.3) | collective-permute-done | bytes 131104 | tf_op jit(solution)/shard_map/ppermute | solution.py:43
  20.0 2.7 %collective-permute-start.6 = (f32[32,512]{1,0:T(8,128)S(1)}, f32[32,512]{1,0:T(8,128)S(1)}, u32[]{:S(2)}, u32[]{:S(2)}) collective-permute-start(f32[32,512]{1,0:T(8,128)S(1)} %slice.33), channel_id=1, source_target_pairs={{0,96},{8,104},{16,112},{24,120},{32,0},{40,8},{48,16},{56,24},{64... | collective-permute-start | bytes 196616 | tf_op jit(solution)/shard_map/ppermute | solution.py:43
  22.8 1.5 collective-permute-done.5
  24.4 1.6 collective-permute-start.7
  26.0 2.2 %collective-permute-start.8 = (f32[256,512]{1,0:T(8,128)S(1)}, f32[256,512]{1,0:T(8,128)S(1)}, u32[]{:S(2)}, u32[]{:S(2)}) collective-permute-start(f32[256,512]{1,0:T(8,128)S(1)} %get-tuple-element.28), channel_id=1, source_target_pairs={{0,24},{8,0},{16,8},{24,16},{32,56},{40,32},{48,40},{56,48},{64,88... | collective-permute-start | bytes 1572872 | tf_op jit(solution)/shard_map/ppermute | solution.py:43
  28.2 22.0 %collective-permute-done.7 = f32[256,512]{1,0:T(8,128)S(1)} collective-permute-done((f32[256,512]{1,0:T(8,128)S(1)}, f32[256,512]{1,0:T(8,128)S(1)}, u32[]{:S(2)}, u32[]{:S(2)}) %collective-permute-start.7) | collective-permute-done | bytes 524320 | tf_op jit(solution)/shard_map/ppermute | solution.py:43
  50.3 3.2 %collective-permute-start.10 = (f32[128,512]{1,0:T(8,128)S(1)}, f32[128,512]{1,0:T(8,128)S(1)}, u32[]{:S(2)}, u32[]{:S(2)}) collective-permute-start(f32[128,512]{1,0:T(8,128)S(1)} %slice.35), channel_id=1, source_target_pairs={{0,24},{8,0},{16,8},{24,16},{32,56},{40,32},{48,40},{56,48},{64,88... | collective-permute-start | bytes 786440 | tf_op jit(solution)/shard_map/ppermute | solution.py:43
  53.6 4.6 %collective-permute-done.9 = f32[128,512]{1,0:T(8,128)S(1)} collective-permute-done((f32[128,512]{1,0:T(8,128)S(1)}, f32[128,512]{1,0:T(8,128)S(1)}, u32[]{:S(2)}, u32[]{:S(2)}) %collective-permute-start.9) | collective-permute-done | bytes 262176 | tf_op jit(solution)/shard_map/ppermute | solution.py:43
  58.3 4.0 %collective-permute-start.11 = (f32[1024,512]{1,0:T(8,128)S(1)}, f32[1024,512]{1,0:T(8,128)S(1)}, u32[]{:S(2)}, u32[]{:S(2)}) collective-permute-start(f32[1024,512]{1,0:T(8,128)S(1)} %constant_dynamic-update-slice_fusion.5.near_ref), channel_id=1, source_target_pairs={{0,2},{2,0},{4,6},{6,4},{1,3},{3,1},{5,7},{7,5},{8,10},{10,8},{12,... | collective-permute-start | bytes 6291464 | tf_op jit(solution)/shard_map/ppermute | solution.py:47
  62.3 1.2 collective-permute-start.1
  63.9 12.0 %collective-permute-done.1.w2 = f32[512,256]{1,0:T(8,128)S(1)} collective-permute-done((f32[512,256]{1,0:T(8,128)S(1)}, f32[512,256]{1,0:T(8,128)S(1)}, u32[]{:S(2)}, u32[]{:S(2)}) %collective-permute-start.1) | collective-permute-done | bytes 524320 | tf_op jit(solution)/shard_map/ppermute | solution.py:47
  76.7 3.2 %copy-done = f32[512,3840]{1,0:T(8,128)S(1)} copy-done((f32[512,3840]{1,0:T(8,128)S(1)}, f32[512,3840]{1,0:T(8,128)}, u32[]{:S(2)}) %copy-start) | copy-done | bytes 7864344
  79.9 6.9 %shard_map.105 = (f32[2,512,128]{2,1,0:T(8,128)S(1)}, f32[2,512,128]{2,1,0:T(8,128)S(1)}) custom-call(s32[5]{0:T(128)S(1)} %copy-done.5, f32[512,256]{1,0:T(8,128)S(1)} %copy-done.3, bf16[512,256]{1,0:T(8,128)(2,1)S(1)} %copy-done.4, f32[512,3840]{1,0:T(8,128)S(1)} %copy-done, bf16[512,3840]{1,0:T(8,128)(2,1)S(1)} %copy-done.1), custom_call_target="tpu_custom_call" | custom-call | flops 2013265920 | bytes 11796480 | tf_op jit(solution)/shard_map/pallas_call | solution.py:246
  87.1 8.6 %shard_map.103 = (bf16[512,1024]{1,0:T(8,128)(2,1)S(1)}, bf16[512,1024]{1,0:T(8,128)(2,1)S(1)}, f32[512,256]{1,0:T(8,128)}) custom-call(s32[5]{0:T(128)S(1)} %copy-done.5, s32[8,8]{1,0:T(8,128)S(1)} %copy-done.6, f32[512,256]{1,0:T(8,128)S(1)} %copy-done.3, f32[512,256]{1,0:T(8,128)S(1)} %collective-permute-done.w1, ...), custom_call_target="tpu_custom_call" | custom-call | flops 6442450944 | bytes 8388608 | tf_op jit(solution)/shard_map/pallas_call | solution.py:314
  95.8 36.2 %all-gather.2.cloned.1.call-done.factor_ref = f32[1024,3840]{1,0:T(8,128)} async-done(((f32[64,3840]{1,0:T(8,128)}), f32[1024,3840]{1,0:T(8,128)}) %all-gather.2.cloned.1.call-update) | async-done | bytes 15728656 | tf_op jit(solution)/shard_map/all_gather | solution.py:298
  131.9 2.1 %copy-done.2 = bf16[512,3840]{1,0:T(8,128)(2,1)S(1)} copy-done((bf16[512,3840]{1,0:T(8,128)(2,1)S(1)}, bf16[512,3840]{1,0:T(8,128)(2,1)}, u32[]{:S(2)}) %copy-start.2) | copy-done | bytes 3932184
  135.1 25.8 %shard_map.104 = (f32[512,3840]{1,0:T(8,128)}, f32[2,512,128]{2,1,0:T(8,128)S(1)}, f32[2,512,128]{2,1,0:T(8,128)S(1)}) custom-call(s32[5]{0:T(128)S(1)} %copy-done.5, f32[512,256]{1,0:T(8,128)S(1)} %copy-done.7, bf16[512,256]{1,0:T(8,128)(2,1)S(1)} %copy-done.4, bf16[512,1024]{1,0:T(8,128)(2,1)S(1)} %get-tuple-element.13.high_ref, ...), custom_call_target="tpu_custom_call" | custom-call | flops 14092861440 | bytes 31457280 | tf_op jit(solution)/shard_map/pallas_call | solution.py:267
  162.8 1.3 collective-permute-start.15
  164.5 6.3 %collective-permute-done.15 = f32[512,128]{1,0:T(8,128)S(1)} collective-permute-done((f32[512,128]{1,0:T(8,128)S(1)}, f32[512,128]{1,0:T(8,128)S(1)}, u32[]{:S(2)}, u32[]{:S(2)}) %collective-permute-start.15) | collective-permute-done | bytes 262176 | tf_op jit(solution)/shard_map/ppermute | solution.py:47
  170.8 5.6 %collective-permute-done.13 = f32[512,128]{1,0:T(8,128)S(1)} collective-permute-done((f32[512,128]{1,0:T(8,128)S(1)}, f32[512,128]{1,0:T(8,128)S(1)}, u32[]{:S(2)}, u32[]{:S(2)}) %collective-permute-start.13) | collective-permute-done | bytes 262176 | tf_op jit(solution)/shard_map/ppermute | solution.py:47
  (51 shorter events, 8.4 us)
Async XLA Ops:
  7.2 124.8 %all-gather.2.cloned.1.call-start = ((), (), s32[]{:S(2)}) async-start(), calls=%async_computation | async-start | bytes 16711680 | tf_op jit(solution)/shard_map/all_gather | solution.py:298
  13.1 6.9 %collective-permute-start.3 = (f32[64,512]{1,0:T(8,128)}, f32[64,512]{1,0:T(8,128)S(1)}, u32[]{:S(2)}, u32[]{:S(2)}) collective-permute-start(f32[64,512]{1,0:T(8,128)} %shard_map.102), channel_id=1, source_target_pairs={{0,32},{8,40},{16,48},{24,56},{32,64},{40,72},{48,80},{56,88},{64,... | collective-permute-start | bytes 393224 | tf_op jit(solution)/shard_map/ppermute | solution.py:43
  15.3 4.7 %collective-permute-start.4 = (f32[64,512]{1,0:T(8,128)}, f32[64,512]{1,0:T(8,128)S(1)}, u32[]{:S(2)}, u32[]{:S(2)}) collective-permute-start(f32[64,512]{1,0:T(8,128)} %shard_map.102), channel_id=1, source_target_pairs={{0,96},{8,104},{16,112},{24,120},{32,0},{40,8},{48,16},{56,24},{64... | collective-permute-start | bytes 393224 | tf_op jit(solution)/shard_map/ppermute | solution.py:43
  20.0 4.3 %collective-permute-start.5 = (f32[32,512]{1,0:T(8,128)S(1)}, f32[32,512]{1,0:T(8,128)S(1)}, u32[]{:S(2)}, u32[]{:S(2)}) collective-permute-start(f32[32,512]{1,0:T(8,128)S(1)} %slice.32), channel_id=1, source_target_pairs={{0,32},{8,40},{16,48},{24,56},{32,64},{40,72},{48,80},{56,88},{64,... | collective-permute-start | bytes 196616 | tf_op jit(solution)/shard_map/ppermute | solution.py:43
  20.0 4.3 %collective-permute-start.6 = (f32[32,512]{1,0:T(8,128)S(1)}, f32[32,512]{1,0:T(8,128)S(1)}, u32[]{:S(2)}, u32[]{:S(2)}) collective-permute-start(f32[32,512]{1,0:T(8,128)S(1)} %slice.33), channel_id=1, source_target_pairs={{0,96},{8,104},{16,112},{24,120},{32,0},{40,8},{48,16},{56,24},{64... | collective-permute-start | bytes 196616 | tf_op jit(solution)/shard_map/ppermute | solution.py:43
  22.8 53.9 %copy-start.4 = (bf16[512,256]{1,0:T(8,128)(2,1)S(1)}, bf16[512,256]{1,0:T(8,128)(2,1)}, u32[]{:S(2)}) copy-start(bf16[512,256]{1,0:T(8,128)(2,1)} %calib_panel_ref.3) | copy-start | bytes 786436
  24.3 38.0 %copy-start.3 = (f32[512,256]{1,0:T(8,128)S(1)}, f32[512,256]{1,0:T(8,128)}, u32[]{:S(2)}) copy-start(f32[512,256]{1,0:T(8,128)} %panel_ref.1) | copy-start | bytes 1572868
  24.4 52.3 %copy-start.1 = (bf16[512,3840]{1,0:T(8,128)(2,1)S(1)}, bf16[512,3840]{1,0:T(8,128)(2,1)}, u32[]{:S(2)}) copy-start(bf16[512,3840]{1,0:T(8,128)(2,1)} %calib_ref.3) | copy-start | bytes 11796484
  24.4 52.3 %copy-start.5 = (s32[5]{0:T(128)S(1)}, s32[5]{0:T(128)}, u32[]{:S(2)}) copy-start(s32[5]{0:T(128)} %stack.23.place) | copy-start | bytes 64
  24.4 25.8 %collective-permute-start.7 = (f32[256,512]{1,0:T(8,128)S(1)}, f32[256,512]{1,0:T(8,128)S(1)}, u32[]{:S(2)}, u32[]{:S(2)}) collective-permute-start(f32[256,512]{1,0:T(8,128)S(1)} %get-tuple-element.28), channel_id=1, source_target_pairs={{0,8},{8,16},{16,24},{24,0},{32,40},{40,48},{48,56},{56,32},{64,72... | collective-permute-start | bytes 1572872 | tf_op jit(solution)/shard_map/ppermute | solution.py:43
  26.0 24.3 %collective-permute-start.8 = (f32[256,512]{1,0:T(8,128)S(1)}, f32[256,512]{1,0:T(8,128)S(1)}, u32[]{:S(2)}, u32[]{:S(2)}) collective-permute-start(f32[256,512]{1,0:T(8,128)S(1)} %get-tuple-element.28), channel_id=1, source_target_pairs={{0,24},{8,0},{16,8},{24,16},{32,56},{40,32},{48,40},{56,48},{64,88... | collective-permute-start | bytes 1572872 | tf_op jit(solution)/shard_map/ppermute | solution.py:43
  50.2 8.0 %collective-permute-start.9 = (f32[128,512]{1,0:T(8,128)S(1)}, f32[128,512]{1,0:T(8,128)S(1)}, u32[]{:S(2)}, u32[]{:S(2)}) collective-permute-start(f32[128,512]{1,0:T(8,128)S(1)} %slice.34), channel_id=1, source_target_pairs={{0,8},{8,16},{16,24},{24,0},{32,40},{40,48},{48,56},{56,32},{64,72... | collective-permute-start | bytes 786440 | tf_op jit(solution)/shard_map/ppermute | solution.py:43
  50.3 7.9 %collective-permute-start.10 = (f32[128,512]{1,0:T(8,128)S(1)}, f32[128,512]{1,0:T(8,128)S(1)}, u32[]{:S(2)}, u32[]{:S(2)}) collective-permute-start(f32[128,512]{1,0:T(8,128)S(1)} %slice.35), channel_id=1, source_target_pairs={{0,24},{8,0},{16,8},{24,16},{32,56},{40,32},{48,40},{56,48},{64,88... | collective-permute-start | bytes 786440 | tf_op jit(solution)/shard_map/ppermute | solution.py:43
  58.2 28.9 %copy-start.6 = (s32[8,8]{1,0:T(8,128)S(1)}, s32[8,8]{1,0:T(8,128)}, u32[]{:S(2)}) copy-start(s32[8,8]{1,0:T(8,128)} %prune_ref.1) | copy-start | bytes 772
  58.3 28.9 %collective-permute-start.11 = (f32[1024,512]{1,0:T(8,128)S(1)}, f32[1024,512]{1,0:T(8,128)S(1)}, u32[]{:S(2)}, u32[]{:S(2)}) collective-permute-start(f32[1024,512]{1,0:T(8,128)S(1)} %constant_dynamic-update-slice_fusion.5.near_ref), channel_id=1, source_target_pairs={{0,2},{2,0},{4,6},{6,4},{1,3},{3,1},{5,7},{7,5},{8,10},{10,8},{12,... | collective-permute-start | bytes 6291464 | tf_op jit(solution)/shard_map/ppermute | solution.py:47
  62.3 13.6 %collective-permute-start.1 = (f32[512,256]{1,0:T(8,128)S(1)}, f32[512,256]{1,0:T(8,128)S(1)}, u32[]{:S(2)}, u32[]{:S(2)}) collective-permute-start(f32[512,256]{1,0:T(8,128)S(1)} %copy-done.3), channel_id=1, source_target_pairs={{0,4},{2,6},{4,0},{6,2},{1,5},{3,7},{5,1},{7,3},{8,12},{10,14},{12... | collective-permute-start | bytes 1572872 | tf_op jit(solution)/shard_map/ppermute | solution.py:47
  63.5 23.6 %collective-permute-start = (f32[512,256]{1,0:T(8,128)S(1)}, f32[512,256]{1,0:T(8,128)S(1)}, u32[]{:S(2)}, u32[]{:S(2)}) collective-permute-start(f32[512,256]{1,0:T(8,128)S(1)} %copy-done.3), channel_id=1, source_target_pairs={{0,2},{2,0},{4,6},{6,4},{1,3},{3,1},{5,7},{7,5},{8,10},{10,8},{12,... | collective-permute-start | bytes 1572872 | tf_op jit(solution)/shard_map/ppermute | solution.py:47
  75.9 11.3 %collective-permute-start.2 = (f32[512,256]{1,0:T(8,128)S(1)}, f32[512,256]{1,0:T(8,128)S(1)}, u32[]{:S(2)}, u32[]{:S(2)}) collective-permute-start(f32[512,256]{1,0:T(8,128)S(1)} %collective-permute-done.1.w2), channel_id=1, source_target_pairs={{0,2},{2,0},{4,6},{6,4},{1,3},{3,1},{5,7},{7,5},{8,10},{10,8},{12,... | collective-permute-start | bytes 1572872 | tf_op jit(solution)/shard_map/ppermute | solution.py:47
  76.7 3.2 %copy-start = (f32[512,3840]{1,0:T(8,128)S(1)}, f32[512,3840]{1,0:T(8,128)}, u32[]{:S(2)}) copy-start(f32[512,3840]{1,0:T(8,128)} %rest_ref.3) | copy-start | bytes 23592964
  86.7 74.9 %collective-permute-start.14 = (f32[2,512,128]{2,1,0:T(8,128)S(1)}, f32[2,512,128]{2,1,0:T(8,128)}, u32[]{:S(2)}, u32[]{:S(2)}) collective-permute-start(f32[2,512,128]{2,1,0:T(8,128)S(1)} %get-tuple-element.19), channel_id=1, source_target_pairs={{0,2},{2,0},{4,6},{6,4},{1,3},{3,1},{5,7},{7,5},{8,10},{10,8},{12,... | collective-permute-start | bytes 1572872 | tf_op jit(solution)/shard_map/ppermute | solution.py:47
  131.9 2.1 %copy-start.2 = (bf16[512,3840]{1,0:T(8,128)(2,1)S(1)}, bf16[512,3840]{1,0:T(8,128)(2,1)}, u32[]{:S(2)}) copy-start(bf16[512,3840]{1,0:T(8,128)(2,1)} %calib_ref.3) | copy-start | bytes 11796484
  160.9 3.1 %collective-permute-start.12 = (f32[2,512,128]{2,1,0:T(8,128)S(1)}, f32[2,512,128]{2,1,0:T(8,128)S(1)}, u32[]{:S(2)}, u32[]{:S(2)}) collective-permute-start(f32[2,512,128]{2,1,0:T(8,128)S(1)} %get-tuple-element.17), channel_id=1, source_target_pairs={{0,2},{2,0},{4,6},{6,4},{1,3},{3,1},{5,7},{7,5},{8,10},{10,8},{12,... | collective-permute-start | bytes 1572872 | tf_op jit(solution)/shard_map/ppermute | solution.py:47
  162.8 8.0 %collective-permute-start.15 = (f32[512,128]{1,0:T(8,128)S(1)}, f32[512,128]{1,0:T(8,128)S(1)}, u32[]{:S(2)}, u32[]{:S(2)}) collective-permute-start(f32[512,128]{1,0:T(8,128)S(1)} %slice_bitcast_fusion), channel_id=1, source_target_pairs={{0,4},{2,6},{4,0},{6,2},{1,5},{3,7},{5,1},{7,3},{8,12},{10,14},{12... | collective-permute-start | bytes 786440 | tf_op jit(solution)/shard_map/ppermute | solution.py:47
  164.1 12.3 %collective-permute-start.13 = (f32[512,128]{1,0:T(8,128)S(1)}, f32[512,128]{1,0:T(8,128)S(1)}, u32[]{:S(2)}, u32[]{:S(2)}) collective-permute-start(f32[512,128]{1,0:T(8,128)S(1)} %slice_bitcast_fusion.2), channel_id=1, source_target_pairs={{0,4},{2,6},{4,0},{6,2},{1,5},{3,7},{5,1},{7,3},{8,12},{10,14},{12... | collective-permute-start | bytes 786440 | tf_op jit(solution)/shard_map/ppermute | solution.py:47
  (1 other events, 1.0 us)
Sparse Core Ops, SparseCore 0:
  10.2 121.6 all-gather.1

commit v2 on v1

--- a/solution.py
+++ b/solution.py
@@ -8,8 +8,11 @@
 from jax.sharding import PartitionSpec as P
 
 BLOCK = 64
+UPDATE_MIB = 56
 RING = 4
 OFFSETS = (0, -1, 1, 2)
+GROUP = 256
+TILE = 768
 F32 = jnp.float32
 BF16 = jnp.bfloat16
 HIGHEST = lax.Precision.HIGHEST
@@ -34,6 +37,14 @@
 
 
 def along(value, axis, step):
+    if axis == "x":
+        pairs = []
+        for x in range(RING):
+            to = (x + step) % RING
+            for core in range(2):
+                pairs.append((((x % 2) * 2 + core) * 2 + x // 2, ((to % 2) * 2 + core) * 2 + to // 2))
+        return lax.ppermute(value, ("cols", "dp"), pairs)
+
     def shift(y, z):
         if axis == "y":
             return ((y + step) % RING) * RING + z
@@ -47,19 +58,36 @@
     return lax.ppermute(value, "cols", [(i, i ^ bit) for i in range(4)])
 
 
-def ring_gather(value, axis):
-    half = value.shape[0] // 2
-    before, after = along(value, axis, 1), along(value, axis, -1)
-    far_top, far_bottom = along(before[:half], axis, 1), along(after[half:], axis, -1)
-    return jnp.concatenate([value, before, after, far_top, far_bottom], axis=0)
-
-
-def factor_kernel(place, diag_ref, rows_ref, out_ref):
+def both_ways(value, axis):
+    return along(value, axis, 1), along(value, axis, -1)
+
+
+def halves(pair):
+    before, after = pair
+    half = before.shape[0] // 2
+    return before[:half], after[half:]
+
+
+def onward(pair, axis):
+    top, bottom = pair
+    return along(top, axis, 1), along(bottom, axis, -1)
+
+
+def after(value, *others):
+    return lax.optimization_barrier((value, others))[0]
+
+
+def rows_of(value):
+    return value.reshape(-1, value.shape[-1])
+
+
+def factor_kernel(place, rows_ref, out_ref):
     block, core = place[0], place[1]
     side = BLOCK
     row = lax.broadcasted_iota(jnp.int32, (side, side), 0)
     column = lax.broadcasted_iota(jnp.int32, (side, side), 1)
-    square = diag_ref[...]
+    pair = rows_ref[:, pl.ds(pl.multiple_of((block >> 1) * 128, 128), 128)]
+    square = jnp.where((block & 1) != 0, pair[:, side:], pair[:, :side])
     identity = (row == column).astype(F32)
     down = jnp.sum(square * identity, axis=1, keepdims=True)
     across = jnp.sum(square * identity, axis=0, keepdims=True)
@@ -70,7 +98,7 @@
         inverse = jnp.dot(inverse, identity + power, precision=HIGHEST, preferred_element_type=F32)
     inverse = inverse / across
     width = out_ref.shape[1]
-    start = pl.multiple_of(core * width, width)
+    start = pl.multiple_of((place[5] * 2 + core) * width, width)
     mine = rows_ref[:, pl.ds(start, width)]
     local = lax.broadcasted_iota(jnp.int32, (side, width), 1) + start - block * side
     wide_row = lax.broadcasted_iota(jnp.int32, (side, width), 0)
@@ -84,21 +112,18 @@
     high_ref, low_ref, kept_ref,
     work, fac_high, fac_low, kept,
 ):
-    col, core, y, z = place[2], place[1], place[3], place[4]
+    col, core, x = place[2], place[1], place[5]
     rows, own = w0.shape
     for slot, piece in enumerate((w0, w1, w2, w3)):
         work[col ^ slot] = piece[...]
-    half = near_ref.shape[1]
+    width = near_ref.shape[-1]
     for which, ref in enumerate((near_ref, far_ref)):
-        start = pl.multiple_of((core ^ which) * half, half)
-        for zi, zo in enumerate(OFFSETS):
-            for yi, yo in enumerate(OFFSETS):
-                block = ((y + yo) & 3) * RING + ((z + zo) & 3)
-                at = (zi * RING + yi) * BLOCK
-                top = pl.multiple_of(block * BLOCK, BLOCK)
-                high, low = split(ref[at : at + BLOCK, :])
-                fac_high[pl.ds(top, BLOCK), pl.ds(start, half)] = high
-                fac_low[pl.ds(top, BLOCK), pl.ds(start, half)] = low
+        for slot, offset in enumerate(OFFSETS):
+            piece = ((x + offset) & 3) * 2 + (core ^ which)
+            start = pl.multiple_of(piece * width, width)
+            high, low = split(ref[slot])
+            fac_high[:, pl.ds(start, width)] = high
+            fac_low[:, pl.ds(start, width)] = low
     groups = rows // BLOCK
     bits = []
     for group in range(groups):
@@ -253,32 +278,30 @@
         out_specs=specs,
         out_shape=shapes,
         scratch_shapes=[pltpu.VMEM((tokens, rows), F32)],
-        compiler_params=params(32),
+        compiler_params=params(16),
         cost_estimate=cost(2 * rows * tokens * columns, rows * columns * 4 + tokens * columns * 2),
     )(place, panel, calib_panel, rest, calib)
 
 
-def update(place, panel, calib_panel, high, low, rest, factor, calib):
+def update(place, panel, calib_panel, errors, rest, factor, calib):
     rows, columns = rest.shape
     tokens = calib.shape[0]
     depth = factor.shape[0]
-    tile = 384
     shapes, specs = slots(rows, tokens)
+    operands = (place, panel, calib_panel, *errors, rest, factor, calib)
     return pl.pallas_call(
         update_kernel,
-        grid=(columns // tile,),
-        in_specs=[
-            SMEM, whole(panel.shape), whole(calib_panel.shape), whole(high.shape), whole(low.shape),
-            tiles(rows, tile), tiles(depth, tile), tiles(tokens, tile),
-        ],
-        out_specs=[tiles(rows, tile)] + specs,
+        grid=(columns // TILE,),
+        in_specs=[SMEM] + [whole(v.shape) for v in operands[1:5]]
+        + [tiles(rows, TILE), tiles(depth, TILE), tiles(tokens, TILE)],
+        out_specs=[tiles(rows, TILE)] + specs,
         out_shape=[jax.ShapeDtypeStruct(rest.shape, F32)] + shapes,
         scratch_shapes=[pltpu.VMEM((tokens, rows), F32)],
-        compiler_params=params(40),
+        compiler_params=params(UPDATE_MIB),
         cost_estimate=cost(
             2 * rows * columns * (3 * depth + tokens), columns * 4 * (2 * rows + depth)
         ),
-    )(place, panel, calib_panel, high, low, rest, factor, calib)
+    )(*operands)
 
 
 def scatter_sum(keep, send):
@@ -292,47 +315,52 @@
     col = lax.axis_index("cols")
     block = lax.axis_index("rows")
     core = col % 2
-    place = jnp.stack([block, core, col, block // RING, block % RING]).astype(jnp.int32)
+    across_x = lax.axis_index("dp") * 2 + col // 2
+    place = jnp.stack([block, core, col, block // RING, block % RING, across_x]).astype(jnp.int32)
     rows, own = panel_weight.shape
     panel = hinv_diag.shape[1]
     gathered = lax.all_gather(hinv_off, "rows", axis=0, tiled=True)
-
-    square = lax.dynamic_slice(hinv_diag, (0, block * BLOCK), (BLOCK, BLOCK))
     mine = pl.pallas_call(
         factor_kernel,
-        in_specs=[SMEM, VMEM, VMEM],
+        in_specs=[SMEM, VMEM],
         out_specs=VMEM,
-        out_shape=jax.ShapeDtypeStruct((BLOCK, panel // 2), F32),
+        out_shape=jax.ShapeDtypeStruct((BLOCK, panel // 8), F32),
         cost_estimate=cost(2 * 64 * 64 * 1600 * 6, 2 * 64 * 1024 * 4),
-    )(place, square, hinv_diag)
-    near = ring_gather(ring_gather(mine, "y"), "z")
+    )(place, hinv_diag)
+
+    part = lax.all_to_all(jnp.broadcast_to(mine[None], (RING * RING, *mine.shape)), "rows", 0, 0)
+    part = part.reshape(panel, panel // 8)
+    across = swap(panel_weight, 2)
+    dense = forward(place, panel_weight, calib_panel, rest_weight, calib_rest)
+    part, across, dense = lax.optimization_barrier((part, across, dense))
+
+    next_x = both_ways(part, "x")
+    pieces = [panel_weight, swap(panel_weight, 1), across]
+    next_x, pieces = lax.optimization_barrier((next_x, pieces))
+    far_x = onward(halves(next_x), "x")
+    pieces.append(swap(across, 1))
+    near = jnp.stack([part, *next_x, jnp.concatenate(far_x)])
     far = swap(near, 1)
-
-    across = swap(panel_weight, 2)
-    pieces = [panel_weight, swap(panel_weight, 1), across, swap(across, 1)]
 
     high, low, kept = pl.pallas_call(
         chain_kernel,
         in_specs=[SMEM, SMEM] + [VMEM] * 6,
         out_specs=[VMEM] * 3,
-        out_shape=[
-            jax.ShapeDtypeStruct((rows, panel), BF16),
-            jax.ShapeDtypeStruct((rows, panel), BF16),
-            jax.ShapeDtypeStruct((rows, own), F32),
-        ],
+        out_shape=[jax.ShapeDtypeStruct((rows, panel), BF16)] * 2
+        + [jax.ShapeDtypeStruct((rows, own), F32)],
         scratch_shapes=[
             pltpu.VMEM((4, rows, own), F32),
             pltpu.VMEM((panel, panel), BF16),
             pltpu.VMEM((panel, panel), BF16),
             pltpu.VMEM((4, rows, own), F32),
         ],
-        compiler_params=params(40),
+        compiler_params=params(24),
         cost_estimate=cost(2 * rows * panel * panel * 6, rows * panel * 8 + panel * panel * 4),
     )(place, prune_blocks, *pieces, near, far)
-
-    dense = scatter_sum(*forward(place, panel_weight, calib_panel, rest_weight, calib_rest))
+    dense = scatter_sum(*dense)
+    gathered, dense = lax.optimization_barrier((gathered, dense))
     new_rest, keep, send = update(
-        place, kept, calib_panel, high, low, rest_weight, gathered, calib_rest
+        place, kept, calib_panel, (high, low), rest_weight, gathered, calib_rest
     )
     pruned = scatter_sum(keep, send)
     return kept, new_rest, pruned.astype(BF16), pruned - dense

time: 184 us -> 167 us (0.908)
  waiting for transfers between devices: 91.2 us -> 74.1 us
    ppermute x8 -> x4, waiting for transfers between devices: 30.4 us -> 18.4 us  [along(): return lax.ppermute(value, ('cols', 'dp'), pairs)]
    ppermute x8 -> x4, starting transfers between devices: 13.4 us -> 3.62 us  [along(): return lax.ppermute(value, ('cols', 'dp'), pairs)]
    all_to_all x0 -> x1, starting transfers between devices: none -> 7.77 us  [on_device(): lax.all_to_all(jnp.broadcast_to(mine[None], (RING * RING, *mine.shape)),...]
    ppermute x8, waiting for transfers between devices: 23.9 us -> 19.5 us  [swap(): return lax.ppermute(value, 'cols', [(i, i ^ bit) for i in range(4)])]
    unnamed x23 -> x18, local copies, waits for them, and re-layouts: 7.5 us -> 8.31 us
  transfers between devices with their start and end apart: 17 -> 14, of which waited for: 8 -> 9; matrix products, arithmetic and copies ran while one was open for 2% -> 2% of each run, Pallas kernels for 24% -> 12%
where the time goes in v2:
time: 167 us
  waiting for transfers between devices  74.1 us (44%)
  Pallas kernels  44.3 us (27%)
  starting transfers between devices  21.5 us (13%)
  between operations  14.2 us (9%)
  local copies, waits for them, and re-layouts  10.7 us (6%)
  other arithmetic  2.16 us (1%)
    all_gather x1, waiting for transfers between devices, on_device(): gathered = lax.all_gather(hinv_off, 'rows', axis=0, tiled=True)  35.5 us
    pallas_call x1, Pallas kernels, update(): pl.pallas_call(update_kernel, grid=(columns // TILE,), in_specs=[SMEM] +...  24.6 us
    ppermute x8, waiting for transfers between devices, swap(): return lax.ppermute(value, 'cols', [(i, i ^ bit) for i in range(4)])  19.5 us
    ppermute x4, waiting for transfers between devices, along(): return lax.ppermute(value, ('cols', 'dp'), pairs)  18.4 us
    ppermute x8, starting transfers between devices, swap(): return lax.ppermute(value, 'cols', [(i, i ^ bit) for i in range(4)])  10.1 us
    pallas_call x1, Pallas kernels, on_device(): pl.pallas_call(chain_kernel, in_specs=[SMEM, SMEM] + [VMEM] * 6, out_spec...  9.7 us
    unnamed x18, local copies, waits for them, and re-layouts  8.31 us
    all_to_all x1, starting transfers between devices, on_device(): lax.all_to_all(jnp.broadcast_to(mine[None], (RING * RING, *mine.shape)),...  7.77 us
  transfers between devices with their start and end apart: 14, of which 9 were waited for; matrix products, arithmetic and copies ran while one was open for 2% of the time, Pallas kernels for 12%

profile of v2, /device:TPU:1, one launch (start us, length us, event | category | flops | bytes accessed | tf_op | source)
XLA Modules:
  0.0 166.9 jit_solution(7560548018367039576)
XLA Ops:
  7.9 2.1 %collective-permute-start = (f32[512,256]{1,0:T(8,128)}, f32[512,256]{1,0:T(8,128)S(1)}, u32[]{:S(2)}, u32[]{:S(2)}) collective-permute-start(f32[512,256]{1,0:T(8,128)} %w0), channel_id=1, source_target_pairs={{0,4},{2,6},{4,0},{6,2},{1,5},{3,7},{5,1},{7,3},{8,12},{10,14},{12... | collective-permute-start | bytes 1572872 | tf_op jit(solution)/shard_map/ppermute | solution.py:58
  10.7 3.1 %shard_map.102 = f32[64,128]{1,0:T(8,128)} custom-call(s32[6]{0:T(128)} %stack.42.place, f32[64,1024]{1,0:T(8,128)} %rows_ref.1), custom_call_target="tpu_custom_call" | custom-call | flops 78643200 | bytes 524288 | tf_op jit(solution)/shard_map/pallas_call | solution.py:323
  13.8 1.6 broadcast_in_dim.2
  15.4 7.8 %all-to-all-start = ((f32[16,64,128]{2,1,0:T(8,128)}), f32[16,64,128]{2,1,0:T(8,128)S(1)}, u32[]{:S(2)}, u32[]{:S(2)}) async-start(f32[16,64,128]{2,1,0:T(8,128)} %broadcast_in_dim.2), calls=%async_computation | async-start | bytes 1048576 | tf_op jit(solution)/shard_map/all_to_all | solution.py:331
  23.2 1.3 collective-permute-start.3
  24.5 3.5 %copy-done = f32[512,3840]{1,0:T(8,128)S(1)} copy-done((f32[512,3840]{1,0:T(8,128)S(1)}, f32[512,3840]{1,0:T(8,128)}, u32[]{:S(2)}) %copy-start) | copy-done | bytes 7864344
  28.1 2.1 %copy-done.1 = bf16[512,3840]{1,0:T(8,128)(2,1)S(1)} copy-done((bf16[512,3840]{1,0:T(8,128)(2,1)S(1)}, bf16[512,3840]{1,0:T(8,128)(2,1)}, u32[]{:S(2)}) %copy-start.1) | copy-done | bytes 3932184
  30.9 6.9 %shard_map.103 = (f32[2,512,128]{2,1,0:T(8,128)S(1)}, f32[2,512,128]{2,1,0:T(8,128)S(1)}) custom-call(s32[6]{0:T(128)S(1)} %copy-done.4, f32[512,256]{1,0:T(8,128)S(1)} %copy-done.2, bf16[512,256]{1,0:T(8,128)(2,1)S(1)} %copy-done.3, f32[512,3840]{1,0:T(8,128)S(1)} %copy-done, bf16[512,3840]{1,0:T(8,128)(2,1)S(1)} %copy-done.1), custom_call_target="tpu_custom_call" | custom-call | flops 2013265920 | bytes 11796480 | tf_op jit(solution)/shard_map/pallas_call | solution.py:271
  37.7 2.1 %collective-permute-start.2 = (f32[1024,128]{1,0:T(8,128)S(1)}, f32[1024,128]{1,0:T(8,128)S(1)}, u32[]{:S(2)}, u32[]{:S(2)}) collective-permute-start(f32[1024,128]{1,0:T(8,128)S(1)} %bitcast.28), channel_id=1, source_target_pairs={{0,5},{2,7},{4,0},{6,2},{1,4},{3,6},{5,1},{7,3},{8,13},{10,15},{12... | collective-permute-start | bytes 1572872 | tf_op jit(solution)/shard_map/ppermute | solution.py:46
  39.8 10.0 %collective-permute-done.2 = f32[1024,128]{1,0:T(8,128)S(1)} collective-permute-done((f32[1024,128]{1,0:T(8,128)S(1)}, f32[1024,128]{1,0:T(8,128)S(1)}, u32[]{:S(2)}, u32[]{:S(2)}) %collective-permute-start.2) | collective-permute-done | bytes 524320 | tf_op jit(solution)/shard_map/ppermute | solution.py:46
  49.9 3.1 %collective-permute-done.1 = f32[1024,128]{1,0:T(8,128)S(1)} collective-permute-done((f32[1024,128]{1,0:T(8,128)S(1)}, f32[1024,128]{1,0:T(8,128)S(1)}, u32[]{:S(2)}, u32[]{:S(2)}) %collective-permute-start.1) | collective-permute-done | bytes 524320 | tf_op jit(solution)/shard_map/ppermute | solution.py:46
  53.4 1.2 collective-permute-start.5
  54.6 3.8 %collective-permute-done.6 = f32[512,128]{1,0:T(8,128)S(1)} collective-permute-done((f32[512,128]{1,0:T(8,128)S(1)}, f32[512,128]{1,0:T(8,128)S(1)}, u32[]{:S(2)}, u32[]{:S(2)}) %collective-permute-start.6) | collective-permute-done | bytes 262176 | tf_op jit(solution)/shard_map/ppermute | solution.py:46
  58.4 1.5 collective-permute-done.5
  60.1 3.6 %collective-permute-start.7 = (f32[4,1024,128]{2,1,0:T(8,128)S(1)}, f32[4,1024,128]{2,1,0:T(8,128)S(1)}, u32[]{:S(2)}, u32[]{:S(2)}) collective-permute-start(f32[4,1024,128]{2,1,0:T(8,128)S(1)} %pad_maximum_fusion.near_ref), channel_id=1, source_target_pairs={{0,2},{2,0},{4,6},{6,4},{1,3},{3,1},{5,7},{7,5},{8,10},{10,8},{12,... | collective-permute-start | bytes 6291464 | tf_op jit(solution)/shard_map/ppermute | solution.py:58
  64.2 4.0 %collective-permute-done.8 = f32[2,512,128]{2,1,0:T(8,128)S(1)} collective-permute-done((f32[2,512,128]{2,1,0:T(8,128)S(1)}, f32[2,512,128]{2,1,0:T(8,128)S(1)}, u32[]{:S(2)}, u32[]{:S(2)}) %collective-permute-start.8) | collective-permute-done | bytes 524320 | tf_op jit(solution)/shard_map/ppermute | solution.py:58
  68.8 7.4 %collective-permute-done.9 = f32[512,128]{1,0:T(8,128)S(1)} collective-permute-done((f32[512,128]{1,0:T(8,128)S(1)}, f32[512,128]{1,0:T(8,128)S(1)}, u32[]{:S(2)}, u32[]{:S(2)}) %collective-permute-start.9) | collective-permute-done | bytes 262176 | tf_op jit(solution)/shard_map/ppermute | solution.py:58
  76.3 9.7 %shard_map.104 = (bf16[512,1024]{1,0:T(8,128)(2,1)S(1)}, bf16[512,1024]{1,0:T(8,128)(2,1)S(1)}, f32[512,256]{1,0:T(8,128)}) custom-call(s32[6]{0:T(128)S(1)} %copy-done.5, s32[8,8]{1,0:T(8,128)S(1)} %copy-done.6, f32[512,256]{1,0:T(8,128)S(1)} %copy-done.2, f32[512,256]{1,0:T(8,128)S(1)} %collective-permute-done.3.w1, ...), custom_call_target="tpu_custom_call" | custom-call | flops 6442450944 | bytes 8388608 | tf_op jit(solution)/shard_map/pallas_call | solution.py:345
  87.9 35.5 %all-gather.2.cloned.1.call-done.factor_ref = f32[1024,3840]{1,0:T(8,128)} async-done(((f32[64,3840]{1,0:T(8,128)}), f32[1024,3840]{1,0:T(8,128)}) %all-gather.2.cloned.1.call-update) | async-done | bytes 15728656 | tf_op jit(solution)/shard_map/all_gather | solution.py:322
  123.4 24.6 %shard_map.105 = (f32[512,3840]{1,0:T(8,128)}, f32[2,512,128]{2,1,0:T(8,128)}, f32[2,512,128]{2,1,0:T(8,128)}) custom-call(s32[6]{0:T(128)} %stack.42.place, f32[512,256]{1,0:T(8,128)} %get-tuple-element.19.panel_ref, bf16[512,256]{1,0:T(8,128)(2,1)} %calib_panel_ref.3, bf16[512,1024]{1,0:T(8,128)(2,1)} %copy-done.7, bf16[512,1024]{1,0:T(8,128)(2,1)} %copy-done.8, ...), custom_call_target="tpu_custom_call" | custom-call | flops 14092861440 | bytes 31457280 | tf_op jit(solution)/shard_map/pallas_call | solution.py:292
  148.8 1.7 %collective-permute-done.10 = f32[2,512,128]{2,1,0:T(8,128)S(1)} collective-permute-done((f32[2,512,128]{2,1,0:T(8,128)}, f32[2,512,128]{2,1,0:T(8,128)S(1)}, u32[]{:S(2)}, u32[]{:S(2)}) %collective-permute-start.10) | collective-permute-done | bytes 524320 | tf_op jit(solution)/shard_map/ppermute | solution.py:58
  150.6 1.1 add.29
  151.7 1.3 collective-permute-start.11
  153.0 6.3 %collective-permute-done.11 = f32[512,128]{1,0:T(8,128)S(1)} collective-permute-done((f32[512,128]{1,0:T(8,128)S(1)}, f32[512,128]{1,0:T(8,128)S(1)}, u32[]{:S(2)}, u32[]{:S(2)}) %collective-permute-start.11) | collective-permute-done | bytes 262176 | tf_op jit(solution)/shard_map/ppermute | solution.py:58
  (39 shorter events, 7.4 us)
Async XLA Ops:
  7.2 16.1 %copy-start.2 = (f32[512,256]{1,0:T(8,128)S(1)}, f32[512,256]{1,0:T(8,128)}, u32[]{:S(2)}) copy-start(f32[512,256]{1,0:T(8,128)} %w0) | copy-start | bytes 1572868
  7.2 17.4 %copy-start.3 = (bf16[512,256]{1,0:T(8,128)(2,1)S(1)}, bf16[512,256]{1,0:T(8,128)(2,1)}, u32[]{:S(2)}) copy-start(bf16[512,256]{1,0:T(8,128)(2,1)} %calib_panel_ref.3) | copy-start | bytes 786436
  7.2 116.2 %all-gather.2.cloned.1.call-start = ((), (), s32[]{:S(2)}) async-start(), calls=%async_computation.1 | async-start | bytes 16711680 | tf_op jit(solution)/shard_map/all_gather | solution.py:322
  7.9 29.8 %collective-permute-start = (f32[512,256]{1,0:T(8,128)}, f32[512,256]{1,0:T(8,128)S(1)}, u32[]{:S(2)}, u32[]{:S(2)}) collective-permute-start(f32[512,256]{1,0:T(8,128)} %w0), channel_id=1, source_target_pairs={{0,4},{2,6},{4,0},{6,2},{1,5},{3,7},{5,1},{7,3},{8,12},{10,14},{12... | collective-permute-start | bytes 1572872 | tf_op jit(solution)/shard_map/ppermute | solution.py:58
  15.4 22.3 %all-to-all-start = ((f32[16,64,128]{2,1,0:T(8,128)}), f32[16,64,128]{2,1,0:T(8,128)S(1)}, u32[]{:S(2)}, u32[]{:S(2)}) async-start(f32[16,64,128]{2,1,0:T(8,128)} %broadcast_in_dim.2), calls=%async_computation | async-start | bytes 1048576 | tf_op jit(solution)/shard_map/all_to_all | solution.py:331
  23.2 16.6 %collective-permute-start.3 = (f32[512,256]{1,0:T(8,128)S(1)}, f32[512,256]{1,0:T(8,128)S(1)}, u32[]{:S(2)}, u32[]{:S(2)}) collective-permute-start(f32[512,256]{1,0:T(8,128)S(1)} %copy-done.2), channel_id=1, source_target_pairs={{0,2},{2,0},{4,6},{6,4},{1,3},{3,1},{5,7},{7,5},{8,10},{10,8},{12,... | collective-permute-start | bytes 1572872 | tf_op jit(solution)/shard_map/ppermute | solution.py:58
  24.5 3.5 %copy-start = (f32[512,3840]{1,0:T(8,128)S(1)}, f32[512,3840]{1,0:T(8,128)}, u32[]{:S(2)}) copy-start(f32[512,3840]{1,0:T(8,128)} %rest_ref.3) | copy-start | bytes 23592964
  28.1 2.1 %copy-start.1 = (bf16[512,3840]{1,0:T(8,128)(2,1)S(1)}, bf16[512,3840]{1,0:T(8,128)(2,1)}, u32[]{:S(2)}) copy-start(bf16[512,3840]{1,0:T(8,128)(2,1)} %calib_ref.3) | copy-start | bytes 11796484
  30.2 0.7 copy-start.4
  37.7 12.1 %collective-permute-start.2 = (f32[1024,128]{1,0:T(8,128)S(1)}, f32[1024,128]{1,0:T(8,128)S(1)}, u32[]{:S(2)}, u32[]{:S(2)}) collective-permute-start(f32[1024,128]{1,0:T(8,128)S(1)} %bitcast.28), channel_id=1, source_target_pairs={{0,5},{2,7},{4,0},{6,2},{1,4},{3,6},{5,1},{7,3},{8,13},{10,15},{12... | collective-permute-start | bytes 1572872 | tf_op jit(solution)/shard_map/ppermute | solution.py:46
  39.8 13.2 %collective-permute-start.1 = (f32[1024,128]{1,0:T(8,128)S(1)}, f32[1024,128]{1,0:T(8,128)S(1)}, u32[]{:S(2)}, u32[]{:S(2)}) collective-permute-start(f32[1024,128]{1,0:T(8,128)S(1)} %bitcast.29), channel_id=1, source_target_pairs={{0,4},{2,6},{4,1},{6,3},{1,5},{3,7},{5,0},{7,2},{8,12},{10,14},{12... | collective-permute-start | bytes 1572872 | tf_op jit(solution)/shard_map/ppermute | solution.py:46
  53.1 5.3 %collective-permute-start.6 = (f32[512,128]{1,0:T(8,128)S(1)}, f32[512,128]{1,0:T(8,128)S(1)}, u32[]{:S(2)}, u32[]{:S(2)}) collective-permute-start(f32[512,128]{1,0:T(8,128)S(1)} %slice.19), channel_id=1, source_target_pairs={{0,5},{2,7},{4,0},{6,2},{1,4},{3,6},{5,1},{7,3},{8,13},{10,15},{12... | collective-permute-start | bytes 786440 | tf_op jit(solution)/shard_map/ppermute | solution.py:46
  53.4 6.4 %collective-permute-start.5 = (f32[512,128]{1,0:T(8,128)S(1)}, f32[512,128]{1,0:T(8,128)S(1)}, u32[]{:S(2)}, u32[]{:S(2)}) collective-permute-start(f32[512,128]{1,0:T(8,128)S(1)} %slice.18), channel_id=1, source_target_pairs={{0,4},{2,6},{4,1},{6,3},{1,5},{3,7},{5,0},{7,2},{8,12},{10,14},{12... | collective-permute-start | bytes 786440 | tf_op jit(solution)/shard_map/ppermute | solution.py:46
  60.0 16.2 %copy-start.5 = (s32[6]{0:T(128)S(1)}, s32[6]{0:T(128)}, u32[]{:S(2)}) copy-start(s32[6]{0:T(128)} %stack.42.place) | copy-start | bytes 76
  60.0 16.2 %copy-start.6 = (s32[8,8]{1,0:T(8,128)S(1)}, s32[8,8]{1,0:T(8,128)}, u32[]{:S(2)}) copy-start(s32[8,8]{1,0:T(8,128)} %prune_ref.1) | copy-start | bytes 772
  60.1 16.2 %collective-permute-start.7 = (f32[4,1024,128]{2,1,0:T(8,128)S(1)}, f32[4,1024,128]{2,1,0:T(8,128)S(1)}, u32[]{:S(2)}, u32[]{:S(2)}) collective-permute-start(f32[4,1024,128]{2,1,0:T(8,128)S(1)} %pad_maximum_fusion.near_ref), channel_id=1, source_target_pairs={{0,2},{2,0},{4,6},{6,4},{1,3},{3,1},{5,7},{7,5},{8,10},{10,8},{12,... | collective-permute-start | bytes 6291464 | tf_op jit(solution)/shard_map/ppermute | solution.py:58
  63.6 4.5 %collective-permute-start.8 = (f32[2,512,128]{2,1,0:T(8,128)S(1)}, f32[2,512,128]{2,1,0:T(8,128)S(1)}, u32[]{:S(2)}, u32[]{:S(2)}) collective-permute-start(f32[2,512,128]{2,1,0:T(8,128)S(1)} %get-tuple-element.36), channel_id=1, source_target_pairs={{0,2},{2,0},{4,6},{6,4},{1,3},{3,1},{5,7},{7,5},{8,10},{10,8},{12,... | collective-permute-start | bytes 1572872 | tf_op jit(solution)/shard_map/ppermute | solution.py:58
  63.7 12.5 %collective-permute-start.4 = (f32[512,256]{1,0:T(8,128)S(1)}, f32[512,256]{1,0:T(8,128)S(1)}, u32[]{:S(2)}, u32[]{:S(2)}) collective-permute-start(f32[512,256]{1,0:T(8,128)S(1)} %collective-permute-done.w2), channel_id=1, source_target_pairs={{0,2},{2,0},{4,6},{6,4},{1,3},{3,1},{5,7},{7,5},{8,10},{10,8},{12,... | collective-permute-start | bytes 1572872 | tf_op jit(solution)/shard_map/ppermute | solution.py:58
  68.3 7.9 %collective-permute-start.9 = (f32[512,128]{1,0:T(8,128)S(1)}, f32[512,128]{1,0:T(8,128)S(1)}, u32[]{:S(2)}, u32[]{:S(2)}) collective-permute-start(f32[512,128]{1,0:T(8,128)S(1)} %slice_bitcast_fusion.2), channel_id=1, source_target_pairs={{0,4},{2,6},{4,0},{6,2},{1,5},{3,7},{5,1},{7,3},{8,12},{10,14},{12... | collective-permute-start | bytes 786440 | tf_op jit(solution)/shard_map/ppermute | solution.py:58
  86.0 1.0 copy-start.7
  86.9 1.0 copy-start.8
  148.0 2.5 %collective-permute-start.10 = (f32[2,512,128]{2,1,0:T(8,128)}, f32[2,512,128]{2,1,0:T(8,128)S(1)}, u32[]{:S(2)}, u32[]{:S(2)}) collective-permute-start(f32[2,512,128]{2,1,0:T(8,128)} %get-tuple-element.40), channel_id=1, source_target_pairs={{0,2},{2,0},{4,6},{6,4},{1,3},{3,1},{5,7},{7,5},{8,10},{10,8},{12,... | collective-permute-start | bytes 1572872 | tf_op jit(solution)/shard_map/ppermute | solution.py:58
  151.7 7.6 %collective-permute-start.11 = (f32[512,128]{1,0:T(8,128)S(1)}, f32[512,128]{1,0:T(8,128)S(1)}, u32[]{:S(2)}, u32[]{:S(2)}) collective-permute-start(f32[512,128]{1,0:T(8,128)S(1)} %slice_bitcast_fusion), channel_id=1, source_target_pairs={{0,4},{2,6},{4,0},{6,2},{1,5},{3,7},{5,1},{7,3},{8,12},{10,14},{12... | collective-permute-start | bytes 786440 | tf_op jit(solution)/shard_map/ppermute | solution.py:58
Sparse Core Ops, SparseCore 0:
  10.2 113.1 all-gather.1

commit v3 on v2

--- a/solution.py
+++ b/solution.py
@@ -8,7 +8,7 @@
 from jax.sharding import PartitionSpec as P
 
 BLOCK = 64
-UPDATE_MIB = 56
+UPDATE_MIB = 53
 RING = 4
 OFFSETS = (0, -1, 1, 2)
 GROUP = 256
@@ -77,8 +77,9 @@
     return lax.optimization_barrier((value, others))[0]
 
 
-def rows_of(value):
-    return value.reshape(-1, value.shape[-1])
+def ring_gather(value, axis):
+    pair = both_ways(value, axis)
+    return jnp.concatenate([value, *pair, *onward(halves(pair), axis)])
 
 
 def factor_kernel(place, rows_ref, out_ref):
@@ -112,7 +113,7 @@
     high_ref, low_ref, kept_ref,
     work, fac_high, fac_low, kept,
 ):
-    col, core, x = place[2], place[1], place[5]
+    col, core, y, z, x = place[2], place[1], place[3], place[4], place[5]
     rows, own = w0.shape
     for slot, piece in enumerate((w0, w1, w2, w3)):
         work[col ^ slot] = piece[...]
@@ -121,9 +122,14 @@
         for slot, offset in enumerate(OFFSETS):
             piece = ((x + offset) & 3) * 2 + (core ^ which)
             start = pl.multiple_of(piece * width, width)
-            high, low = split(ref[slot])
-            fac_high[:, pl.ds(start, width)] = high
-            fac_low[:, pl.ds(start, width)] = low
+            for outer, zo in enumerate(OFFSETS):
+                for inner, yo in enumerate(OFFSETS):
+                    block = ((y + yo) & 3) * RING + ((z + zo) & 3)
+                    top = pl.multiple_of(block * BLOCK, BLOCK)
+                    at = (outer * RING + inner) * BLOCK
+                    high, low = split(ref[slot, at : at + BLOCK, :])
+                    fac_high[pl.ds(top, BLOCK), pl.ds(start, width)] = high
+                    fac_low[pl.ds(top, BLOCK), pl.ds(start, width)] = low
     groups = rows // BLOCK
     bits = []
     for group in range(groups):
@@ -191,20 +197,19 @@
     kept_ref[...] = kept[col]
 
 
-def store_slots(place, total, keep_ref, send_ref):
+def store_slots(place, total, refs):
     col = place[2]
-    width = keep_ref.shape[2]
-    for slot in range(4):
-        ref = send_ref if slot & 1 else keep_ref
+    width = refs[0].shape[1]
+    for slot, ref in enumerate(refs):
         group = col ^ slot
         for source in range(4):
 
             @pl.when(group == source)
             def _():
-                ref[slot >> 1] = total[:, source * width : (source + 1) * width]
-
-
-def forward_kernel(place, panel_ref, calib_panel_ref, rest_ref, calib_ref, keep_ref, send_ref, total):
+                ref[...] = total[:, source * width : (source + 1) * width]
+
+
+def forward_kernel(place, panel_ref, calib_panel_ref, rest_ref, calib_ref, k0, s0, k1, s1, total):
     step = pl.program_id(0)
 
     @pl.when(step == 0)
@@ -215,12 +220,12 @@
 
     @pl.when(step == pl.num_programs(0) - 1)
     def _():
-        store_slots(place, total, keep_ref, send_ref)
+        store_slots(place, total, (k0, s0, k1, s1))
 
 
 def update_kernel(
     place, panel_ref, calib_panel_ref, high_ref, low_ref, rest_ref, factor_ref, calib_ref,
-    new_ref, keep_ref, send_ref, total,
+    new_ref, k0, s0, k1, s1, total,
 ):
     step = pl.program_id(0)
 
@@ -234,7 +239,7 @@
 
     @pl.when(step == pl.num_programs(0) - 1)
     def _():
-        store_slots(place, total, keep_ref, send_ref)
+        store_slots(place, total, (k0, s0, k1, s1))
 
 
 SMEM = pl.BlockSpec(memory_space=pltpu.SMEM)
@@ -250,9 +255,8 @@
 
 
 def slots(rows, tokens):
-    shape = jax.ShapeDtypeStruct((2, tokens, rows // 4), F32)
-    spec = pl.BlockSpec((2, tokens, rows // 4), lambda i: (0, 0, 0))
-    return [shape, shape], [spec, spec]
+    shape = jax.ShapeDtypeStruct((tokens, rows // 4), F32)
+    return [shape] * 4, [whole(shape.shape)] * 4
 
 
 def whole(shape):
@@ -304,9 +308,10 @@
     )(*operands)
 
 
-def scatter_sum(keep, send):
-    near = keep + swap(send, 1)
-    return near[0] + swap(near[1], 2)
+def scatter_sum(k0, s0, k1, s1):
+    ahead = swap(s1, 1)
+    stays = swap(s0, 1)
+    return k0 + stays + swap(k1 + ahead, 2)
 
 
 def on_device(
@@ -328,8 +333,7 @@
         cost_estimate=cost(2 * 64 * 64 * 1600 * 6, 2 * 64 * 1024 * 4),
     )(place, hinv_diag)
 
-    part = lax.all_to_all(jnp.broadcast_to(mine[None], (RING * RING, *mine.shape)), "rows", 0, 0)
-    part = part.reshape(panel, panel // 8)
+    part = ring_gather(ring_gather(mine, "y"), "z")
     across = swap(panel_weight, 2)
     dense = forward(place, panel_weight, calib_panel, rest_weight, calib_rest)
     part, across, dense = lax.optimization_barrier((part, across, dense))
@@ -359,10 +363,10 @@
     )(place, prune_blocks, *pieces, near, far)
     dense = scatter_sum(*dense)
     gathered, dense = lax.optimization_barrier((gathered, dense))
-    new_rest, keep, send = update(
+    new_rest, *parts = update(
         place, kept, calib_panel, (high, low), rest_weight, gathered, calib_rest
     )
-    pruned = scatter_sum(keep, send)
+    pruned = scatter_sum(*parts)
     return kept, new_rest, pruned.astype(BF16), pruned - dense
 
 

time: 167 us -> 165 us (0.988)
  waiting for transfers between devices: 74.1 us -> 66.6 us
  starting transfers between devices: 21.5 us -> 28.4 us
    ppermute x0 -> x8, starting transfers between devices: none -> 13.3 us  [along(): return lax.ppermute(value, 'rows', pairs)]
    all_gather x1, waiting for transfers between devices: 35.5 us -> 22.6 us  [on_device(): gathered = lax.all_gather(hinv_off, 'rows', axis=0, tiled=True)]
    ppermute x0 -> x8, waiting for transfers between devices: none -> 8.05 us  [along(): return lax.ppermute(value, 'rows', pairs)]
    all_to_all x1 -> x0, starting transfers between devices: 7.77 us -> none  [on_device(): lax.all_to_all(jnp.broadcast_to(mine[None], (RING * RING, *mine.shape)),...]
    ppermute x4, waiting for transfers between devices: 18.4 us -> 16.5 us  [along(): return lax.ppermute(value, ('cols', 'dp'), pairs)]
    ppermute x8 -> x10, starting transfers between devices: 10.1 us -> 11.7 us  [swap(): return lax.ppermute(value, 'cols', [(i, i ^ bit) for i in range(4)])]
    unnamed x18 -> x25, local copies, waits for them, and re-layouts: 8.31 us -> 9.85 us
    ppermute x8 -> x10, waiting for transfers between devices: 19.5 us -> 18.8 us  [swap(): return lax.ppermute(value, 'cols', [(i, i ^ bit) for i in range(4)])]
  transfers between devices with their start and end apart: 14 -> 23, of which waited for: 9 -> 12; matrix products, arithmetic and copies ran while one was open for 2% -> 1% of each run, Pallas kernels for 12% -> 12%
where the time goes in v3:
time: 165 us; the launch traced here: 164 us
  waiting for transfers between devices  66.6 us (40%)
  Pallas kernels  43.5 us (26%)
  starting transfers between devices  28.4 us (17%)
  between operations  14.3 us (9%)
  local copies, waits for them, and re-layouts  10.5 us (6%)
    pallas_call x1, Pallas kernels, update(): pl.pallas_call(update_kernel, grid=(columns // TILE,), in_specs=[SMEM] +...  24.3 us
    all_gather x1, waiting for transfers between devices, on_device(): gathered = lax.all_gather(hinv_off, 'rows', axis=0, tiled=True)  22.6 us
    ppermute x10, waiting for transfers between devices, swap(): return lax.ppermute(value, 'cols', [(i, i ^ bit) for i in range(4)])  18.8 us
    ppermute x4, waiting for transfers between devices, along(): return lax.ppermute(value, ('cols', 'dp'), pairs)  16.5 us
    ppermute x8, starting transfers between devices, along(): return lax.ppermute(value, 'rows', pairs)  13.3 us
    ppermute x10, starting transfers between devices, swap(): return lax.ppermute(value, 'cols', [(i, i ^ bit) for i in range(4)])  11.7 us
    unnamed x25, local copies, waits for them, and re-layouts  9.85 us
    pallas_call x1, Pallas kernels, on_device(): pl.pallas_call(chain_kernel, in_specs=[SMEM, SMEM] + [VMEM] * 6, out_spec...  9.15 us
  transfers between devices with their start and end apart: 23, of which 12 were waited for; matrix products, arithmetic and copies ran while one was open for 1% of the time, Pallas kernels for 12%

profile of v3, /device:TPU:1, one launch (start us, length us, event | category | flops | bytes accessed | tf_op | source)
XLA Modules:
  0.0 164.3 jit_solution(15967503600571583654)
XLA Ops:
  8.5 3.1 %shard_map.102 = f32[64,128]{1,0:T(8,128)} custom-call(s32[6]{0:T(128)} %stack.42.place, f32[64,1024]{1,0:T(8,128)} %rows_ref.1), custom_call_target="tpu_custom_call" | custom-call | flops 78643200 | bytes 524288 | tf_op jit(solution)/shard_map/pallas_call | solution.py:328
  11.7 3.6 %collective-permute-start.1 = (f32[64,128]{1,0:T(8,128)}, f32[64,128]{1,0:T(8,128)S(1)}, u32[]{:S(2)}, u32[]{:S(2)}) collective-permute-start(f32[64,128]{1,0:T(8,128)} %shard_map.102), channel_id=1, source_target_pairs={{0,96},{8,104},{16,112},{24,120},{32,0},{40,8},{48,16},{56,24},{64... | collective-permute-start | bytes 98312 | tf_op jit(solution)/shard_map/ppermute | solution.py:54
  18.4 3.0 %collective-permute-start.3 = (f32[32,128]{1,0:T(8,128)S(1)}, f32[32,128]{1,0:T(8,128)S(1)}, u32[]{:S(2)}, u32[]{:S(2)}) collective-permute-start(f32[32,128]{1,0:T(8,128)S(1)} %slice.25), channel_id=1, source_target_pairs={{0,96},{8,104},{16,112},{24,120},{32,0},{40,8},{48,16},{56,24},{64... | collective-permute-start | bytes 49160 | tf_op jit(solution)/shard_map/ppermute | solution.py:54
  21.5 3.8 %collective-permute-done.2 = f32[32,128]{1,0:T(8,128)S(1)} collective-permute-done((f32[32,128]{1,0:T(8,128)S(1)}, f32[32,128]{1,0:T(8,128)S(1)}, u32[]{:S(2)}, u32[]{:S(2)}) %collective-permute-start.2) | collective-permute-done | bytes 16416 | tf_op jit(solution)/shard_map/ppermute | solution.py:54
  25.3 3.8 %collective-permute-start.5 = (f32[256,128]{1,0:T(8,128)S(1)}, f32[256,128]{1,0:T(8,128)S(1)}, u32[]{:S(2)}, u32[]{:S(2)}) collective-permute-start(f32[256,128]{1,0:T(8,128)S(1)} %get-tuple-element.62), channel_id=1, source_target_pairs={{0,24},{8,0},{16,8},{24,16},{32,56},{40,32},{48,40},{56,48},{64,88... | collective-permute-start | bytes 393224 | tf_op jit(solution)/shard_map/ppermute | solution.py:54
  29.1 3.4 %copy-done = f32[512,3840]{1,0:T(8,128)S(1)} copy-done((f32[512,3840]{1,0:T(8,128)S(1)}, f32[512,3840]{1,0:T(8,128)}, u32[]{:S(2)}) %copy-start) | copy-done | bytes 7864344
  32.5 2.1 %copy-done.1 = bf16[512,3840]{1,0:T(8,128)(2,1)S(1)} copy-done((bf16[512,3840]{1,0:T(8,128)(2,1)S(1)}, bf16[512,3840]{1,0:T(8,128)(2,1)}, u32[]{:S(2)}) %copy-start.1) | copy-done | bytes 3932184
  36.2 6.9 %shard_map.103 = (f32[512,128]{1,0:T(8,128)S(1)}, f32[512,128]{1,0:T(8,128)S(1)}, f32[512,128]{1,0:T(8,128)S(1)}, f32[512,128]{1,0:T(8,128)S(1)}) custom-call(s32[6]{0:T(128)S(1)} %copy-done.4, f32[512,256]{1,0:T(8,128)S(1)} %copy-done.2, bf16[512,256]{1,0:T(8,128)(2,1)S(1)} %copy-done.3, f32[512,3840]{1,0:T(8,128)S(1)} %copy-done, ...), custom_call_target="tpu_custom_call" | custom-call | flops 2013265920 | bytes 11796480 | tf_op jit(solution)/shard_map/pallas_call | solution.py:275
  43.0 2.8 %collective-permute-start.7 = (f32[128,128]{1,0:T(8,128)S(1)}, f32[128,128]{1,0:T(8,128)S(1)}, u32[]{:S(2)}, u32[]{:S(2)}) collective-permute-start(f32[128,128]{1,0:T(8,128)S(1)} %slice.27), channel_id=1, source_target_pairs={{0,24},{8,0},{16,8},{24,16},{32,56},{40,32},{48,40},{56,48},{64,88... | collective-permute-start | bytes 196616 | tf_op jit(solution)/shard_map/ppermute | solution.py:54
  46.0 4.3 %collective-permute-done.6 = f32[128,128]{1,0:T(8,128)S(1)} collective-permute-done((f32[128,128]{1,0:T(8,128)S(1)}, f32[128,128]{1,0:T(8,128)S(1)}, u32[]{:S(2)}, u32[]{:S(2)}) %collective-permute-start.6) | collective-permute-done | bytes 65568 | tf_op jit(solution)/shard_map/ppermute | solution.py:54
  50.3 1.8 %collective-permute-start.10 = (f32[1024,128]{1,0:T(8,128)S(1)}, f32[1024,128]{1,0:T(8,128)S(1)}, u32[]{:S(2)}, u32[]{:S(2)}) collective-permute-start(f32[1024,128]{1,0:T(8,128)S(1)} %constant_dynamic-update-slice_fusion.5), channel_id=1, source_target_pairs={{0,5},{2,7},{4,0},{6,2},{1,4},{3,6},{5,1},{7,3},{8,13},{10,15},{12... | collective-permute-start | bytes 1572872 | tf_op jit(solution)/shard_map/ppermute | solution.py:46
  52.1 8.3 %collective-permute-done.10 = f32[1024,128]{1,0:T(8,128)S(1)} collective-permute-done((f32[1024,128]{1,0:T(8,128)S(1)}, f32[1024,128]{1,0:T(8,128)S(1)}, u32[]{:S(2)}, u32[]{:S(2)}) %collective-permute-start.10) | collective-permute-done | bytes 524320 | tf_op jit(solution)/shard_map/ppermute | solution.py:46
  60.5 2.2 %collective-permute-done.9 = f32[1024,128]{1,0:T(8,128)S(1)} collective-permute-done((f32[1024,128]{1,0:T(8,128)S(1)}, f32[1024,128]{1,0:T(8,128)S(1)}, u32[]{:S(2)}, u32[]{:S(2)}) %collective-permute-start.9) | collective-permute-done | bytes 524320 | tf_op jit(solution)/shard_map/ppermute | solution.py:46
  64.3 4.2 %collective-permute-done.14 = f32[512,128]{1,0:T(8,128)S(1)} collective-permute-done((f32[512,128]{1,0:T(8,128)S(1)}, f32[512,128]{1,0:T(8,128)S(1)}, u32[]{:S(2)}, u32[]{:S(2)}) %collective-permute-start.14) | collective-permute-done | bytes 262176 | tf_op jit(solution)/shard_map/ppermute | solution.py:46
  68.5 1.7 %collective-permute-done.13 = f32[512,128]{1,0:T(8,128)S(1)} collective-permute-done((f32[512,128]{1,0:T(8,128)S(1)}, f32[512,128]{1,0:T(8,128)S(1)}, u32[]{:S(2)}, u32[]{:S(2)}) %collective-permute-start.13) | collective-permute-done | bytes 262176 | tf_op jit(solution)/shard_map/ppermute | solution.py:46
  70.4 6.3 %collective-permute-start.15 = (f32[4,1024,128]{2,1,0:T(8,128)S(1)}, f32[4,1024,128]{2,1,0:T(8,128)S(1)}, u32[]{:S(2)}, u32[]{:S(2)}) collective-permute-start(f32[4,1024,128]{2,1,0:T(8,128)S(1)} %pad_maximum_fusion.near_ref), channel_id=1, source_target_pairs={{0,2},{2,0},{4,6},{6,4},{1,3},{3,1},{5,7},{7,5},{8,10},{10,8},{12,... | collective-permute-start | bytes 6291464 | tf_op jit(solution)/shard_map/ppermute | solution.py:58
  77.3 3.6 %collective-permute-done.17 = f32[512,128]{1,0:T(8,128)S(1)} collective-permute-done((f32[512,128]{1,0:T(8,128)S(1)}, f32[512,128]{1,0:T(8,128)S(1)}, u32[]{:S(2)}, u32[]{:S(2)}) %collective-permute-start.17) | collective-permute-done | bytes 262176 | tf_op jit(solution)/shard_map/ppermute | solution.py:58
  82.0 6.8 %collective-permute-done.18 = f32[512,128]{1,0:T(8,128)S(1)} collective-permute-done((f32[512,128]{1,0:T(8,128)S(1)}, f32[512,128]{1,0:T(8,128)S(1)}, u32[]{:S(2)}, u32[]{:S(2)}) %collective-permute-start.18) | collective-permute-done | bytes 262176 | tf_op jit(solution)/shard_map/ppermute | solution.py:58
  88.8 9.2 %shard_map.104 = (bf16[512,1024]{1,0:T(8,128)(2,1)S(1)}, bf16[512,1024]{1,0:T(8,128)(2,1)S(1)}, f32[512,256]{1,0:T(8,128)}) custom-call(s32[6]{0:T(128)S(1)} %copy-done.5, s32[8,8]{1,0:T(8,128)S(1)} %copy-done.6, f32[512,256]{1,0:T(8,128)S(1)} %copy-done.2, f32[512,256]{1,0:T(8,128)S(1)} %collective-permute-done.11.w1, ...), custom_call_target="tpu_custom_call" | custom-call | flops 6442450944 | bytes 8388608 | tf_op jit(solution)/shard_map/pallas_call | solution.py:349
  100.0 22.6 %all-gather.2.cloned.1.call-done.factor_ref = f32[1024,3840]{1,0:T(8,128)} async-done(((f32[64,3840]{1,0:T(8,128)}), f32[1024,3840]{1,0:T(8,128)}) %all-gather.2.cloned.1.call-update) | async-done | bytes 15728656 | tf_op jit(solution)/shard_map/all_gather | solution.py:327
  122.6 24.3 %shard_map.105 = (f32[512,3840]{1,0:T(8,128)}, f32[512,128]{1,0:T(8,128)S(1)}, f32[512,128]{1,0:T(8,128)S(1)}, f32[512,128]{1,0:T(8,128)S(1)}, f32[512,128]{1,0:T(8,128)}) custom-call(s32[6]{0:T(128)S(1)} %copy-done.5, f32[512,256]{1,0:T(8,128)} %get-tuple-element.25.panel_ref, bf16[512,256]{1,0:T(8,128)(2,1)} %calib_panel_ref.3, ...), custom_call_target="tpu_custom_call" | custom-call | flops 14092861440 | bytes 31457280 | tf_op jit(solution)/shard_map/pallas_call | solution.py:296
  147.8 1.3 collective-permute-done.20
  149.1 1.3 collective-permute-start.21
  150.4 6.3 %collective-permute-done.21 = f32[512,128]{1,0:T(8,128)S(1)} collective-permute-done((f32[512,128]{1,0:T(8,128)S(1)}, f32[512,128]{1,0:T(8,128)S(1)}, u32[]{:S(2)}, u32[]{:S(2)}) %collective-permute-start.21) | collective-permute-done | bytes 262176 | tf_op jit(solution)/shard_map/ppermute | solution.py:58
  (67 shorter events, 13.4 us)
Async XLA Ops:
  7.2 21.9 %copy-start.2 = (f32[512,256]{1,0:T(8,128)S(1)}, f32[512,256]{1,0:T(8,128)}, u32[]{:S(2)}) copy-start(f32[512,256]{1,0:T(8,128)} %w0) | copy-start | bytes 1572868
  7.2 115.4 %all-gather.2.cloned.1.call-start = ((), (), s32[]{:S(2)}) async-start(), calls=%async_computation | async-start | bytes 16711680 | tf_op jit(solution)/shard_map/all_gather | solution.py:327
  11.7 6.8 %collective-permute-start.1 = (f32[64,128]{1,0:T(8,128)}, f32[64,128]{1,0:T(8,128)S(1)}, u32[]{:S(2)}, u32[]{:S(2)}) collective-permute-start(f32[64,128]{1,0:T(8,128)} %shard_map.102), channel_id=1, source_target_pairs={{0,96},{8,104},{16,112},{24,120},{32,0},{40,8},{48,16},{56,24},{64... | collective-permute-start | bytes 98312 | tf_op jit(solution)/shard_map/ppermute | solution.py:54
  15.2 6.3 %collective-permute-start = (f32[64,128]{1,0:T(8,128)}, f32[64,128]{1,0:T(8,128)S(1)}, u32[]{:S(2)}, u32[]{:S(2)}) collective-permute-start(f32[64,128]{1,0:T(8,128)} %shard_map.102), channel_id=1, source_target_pairs={{0,32},{8,40},{16,48},{24,56},{32,64},{40,72},{48,80},{56,88},{64,... | collective-permute-start | bytes 98312 | tf_op jit(solution)/shard_map/ppermute | solution.py:54
  15.2 35.1 %collective-permute-start.8 = (f32[512,256]{1,0:T(8,128)}, f32[512,256]{1,0:T(8,128)S(1)}, u32[]{:S(2)}, u32[]{:S(2)}) collective-permute-start(f32[512,256]{1,0:T(8,128)} %w0), channel_id=1, source_target_pairs={{0,4},{2,6},{4,0},{6,2},{1,5},{3,7},{5,1},{7,3},{8,12},{10,14},{12... | collective-permute-start | bytes 1572872 | tf_op jit(solution)/shard_map/ppermute | solution.py:58
  16.4 35.7 %collective-permute-start.11 = (f32[512,256]{1,0:T(8,128)}, f32[512,256]{1,0:T(8,128)S(1)}, u32[]{:S(2)}, u32[]{:S(2)}) collective-permute-start(f32[512,256]{1,0:T(8,128)} %w0), channel_id=1, source_target_pairs={{0,2},{2,0},{4,6},{6,4},{1,3},{3,1},{5,7},{7,5},{8,10},{10,8},{12,... | collective-permute-start | bytes 1572872 | tf_op jit(solution)/shard_map/ppermute | solution.py:58
  18.4 6.8 %collective-permute-start.3 = (f32[32,128]{1,0:T(8,128)S(1)}, f32[32,128]{1,0:T(8,128)S(1)}, u32[]{:S(2)}, u32[]{:S(2)}) collective-permute-start(f32[32,128]{1,0:T(8,128)S(1)} %slice.25), channel_id=1, source_target_pairs={{0,96},{8,104},{16,112},{24,120},{32,0},{40,8},{48,16},{56,24},{64... | collective-permute-start | bytes 49160 | tf_op jit(solution)/shard_map/ppermute | solution.py:54
  21.5 3.8 %collective-permute-start.2 = (f32[32,128]{1,0:T(8,128)S(1)}, f32[32,128]{1,0:T(8,128)S(1)}, u32[]{:S(2)}, u32[]{:S(2)}) collective-permute-start(f32[32,128]{1,0:T(8,128)S(1)} %slice.24), channel_id=1, source_target_pairs={{0,32},{8,40},{16,48},{24,56},{32,64},{40,72},{48,80},{56,88},{64,... | collective-permute-start | bytes 49160 | tf_op jit(solution)/shard_map/ppermute | solution.py:54
  25.3 17.7 %collective-permute-start.5 = (f32[256,128]{1,0:T(8,128)S(1)}, f32[256,128]{1,0:T(8,128)S(1)}, u32[]{:S(2)}, u32[]{:S(2)}) collective-permute-start(f32[256,128]{1,0:T(8,128)S(1)} %get-tuple-element.62), channel_id=1, source_target_pairs={{0,24},{8,0},{16,8},{24,16},{32,56},{40,32},{48,40},{56,48},{64,88... | collective-permute-start | bytes 393224 | tf_op jit(solution)/shard_map/ppermute | solution.py:54
  29.1 16.8 %collective-permute-start.4 = (f32[256,128]{1,0:T(8,128)S(1)}, f32[256,128]{1,0:T(8,128)S(1)}, u32[]{:S(2)}, u32[]{:S(2)}) collective-permute-start(f32[256,128]{1,0:T(8,128)S(1)} %get-tuple-element.62), channel_id=1, source_target_pairs={{0,8},{8,16},{16,24},{24,0},{32,40},{40,48},{48,56},{56,32},{64,72... | collective-permute-start | bytes 393224 | tf_op jit(solution)/shard_map/ppermute | solution.py:54
  43.0 7.2 %collective-permute-start.7 = (f32[128,128]{1,0:T(8,128)S(1)}, f32[128,128]{1,0:T(8,128)S(1)}, u32[]{:S(2)}, u32[]{:S(2)}) collective-permute-start(f32[128,128]{1,0:T(8,128)S(1)} %slice.27), channel_id=1, source_target_pairs={{0,24},{8,0},{16,8},{24,16},{32,56},{40,32},{48,40},{56,48},{64,88... | collective-permute-start | bytes 196616 | tf_op jit(solution)/shard_map/ppermute | solution.py:54
  45.9 4.4 %collective-permute-start.6 = (f32[128,128]{1,0:T(8,128)S(1)}, f32[128,128]{1,0:T(8,128)S(1)}, u32[]{:S(2)}, u32[]{:S(2)}) collective-permute-start(f32[128,128]{1,0:T(8,128)S(1)} %slice.26), channel_id=1, source_target_pairs={{0,8},{8,16},{16,24},{24,0},{32,40},{40,48},{48,56},{56,32},{64,72... | collective-permute-start | bytes 196616 | tf_op jit(solution)/shard_map/ppermute | solution.py:54
  50.3 10.2 %collective-permute-start.10 = (f32[1024,128]{1,0:T(8,128)S(1)}, f32[1024,128]{1,0:T(8,128)S(1)}, u32[]{:S(2)}, u32[]{:S(2)}) collective-permute-start(f32[1024,128]{1,0:T(8,128)S(1)} %constant_dynamic-update-slice_fusion.5), channel_id=1, source_target_pairs={{0,5},{2,7},{4,0},{6,2},{1,4},{3,6},{5,1},{7,3},{8,13},{10,15},{12... | collective-permute-start | bytes 1572872 | tf_op jit(solution)/shard_map/ppermute | solution.py:46
  52.1 10.6 %collective-permute-start.9 = (f32[1024,128]{1,0:T(8,128)S(1)}, f32[1024,128]{1,0:T(8,128)S(1)}, u32[]{:S(2)}, u32[]{:S(2)}) collective-permute-start(f32[1024,128]{1,0:T(8,128)S(1)} %constant_dynamic-update-slice_fusion.5), channel_id=1, source_target_pairs={{0,4},{2,6},{4,1},{6,3},{1,5},{3,7},{5,0},{7,2},{8,12},{10,14},{12... | collective-permute-start | bytes 1572872 | tf_op jit(solution)/shard_map/ppermute | solution.py:46
  62.8 5.7 %collective-permute-start.14 = (f32[512,128]{1,0:T(8,128)S(1)}, f32[512,128]{1,0:T(8,128)S(1)}, u32[]{:S(2)}, u32[]{:S(2)}) collective-permute-start(f32[512,128]{1,0:T(8,128)S(1)} %slice.23), channel_id=1, source_target_pairs={{0,5},{2,7},{4,0},{6,2},{1,4},{3,6},{5,1},{7,3},{8,13},{10,15},{12... | collective-permute-start | bytes 786440 | tf_op jit(solution)/shard_map/ppermute | solution.py:46
  63.1 7.1 %collective-permute-start.13 = (f32[512,128]{1,0:T(8,128)S(1)}, f32[512,128]{1,0:T(8,128)S(1)}, u32[]{:S(2)}, u32[]{:S(2)}) collective-permute-start(f32[512,128]{1,0:T(8,128)S(1)} %slice.22), channel_id=1, source_target_pairs={{0,4},{2,6},{4,1},{6,3},{1,5},{3,7},{5,0},{7,2},{8,12},{10,14},{12... | collective-permute-start | bytes 786440 | tf_op jit(solution)/shard_map/ppermute | solution.py:46
  70.4 18.4 %collective-permute-start.15 = (f32[4,1024,128]{2,1,0:T(8,128)S(1)}, f32[4,1024,128]{2,1,0:T(8,128)S(1)}, u32[]{:S(2)}, u32[]{:S(2)}) collective-permute-start(f32[4,1024,128]{2,1,0:T(8,128)S(1)} %pad_maximum_fusion.near_ref), channel_id=1, source_target_pairs={{0,2},{2,0},{4,6},{6,4},{1,3},{3,1},{5,7},{7,5},{8,10},{10,8},{12,... | collective-permute-start | bytes 6291464 | tf_op jit(solution)/shard_map/ppermute | solution.py:58
  76.7 4.2 %collective-permute-start.17 = (f32[512,128]{1,0:T(8,128)S(1)}, f32[512,128]{1,0:T(8,128)S(1)}, u32[]{:S(2)}, u32[]{:S(2)}) collective-permute-start(f32[512,128]{1,0:T(8,128)S(1)} %get-tuple-element.46), channel_id=1, source_target_pairs={{0,2},{2,0},{4,6},{6,4},{1,3},{3,1},{5,7},{7,5},{8,10},{10,8},{12,... | collective-permute-start | bytes 786440 | tf_op jit(solution)/shard_map/ppermute | solution.py:58
  76.8 12.0 %collective-permute-start.12 = (f32[512,256]{1,0:T(8,128)S(1)}, f32[512,256]{1,0:T(8,128)S(1)}, u32[]{:S(2)}, u32[]{:S(2)}) collective-permute-start(f32[512,256]{1,0:T(8,128)S(1)} %collective-permute-done.8.w2), channel_id=1, source_target_pairs={{0,2},{2,0},{4,6},{6,4},{1,3},{3,1},{5,7},{7,5},{8,10},{10,8},{12,... | collective-permute-start | bytes 1572872 | tf_op jit(solution)/shard_map/ppermute | solution.py:58
  77.2 4.8 %collective-permute-start.16 = (f32[512,128]{1,0:T(8,128)S(1)}, f32[512,128]{1,0:T(8,128)S(1)}, u32[]{:S(2)}, u32[]{:S(2)}) collective-permute-start(f32[512,128]{1,0:T(8,128)S(1)} %get-tuple-element.44), channel_id=1, source_target_pairs={{0,2},{2,0},{4,6},{6,4},{1,3},{3,1},{5,7},{7,5},{8,10},{10,8},{12,... | collective-permute-start | bytes 786440 | tf_op jit(solution)/shard_map/ppermute | solution.py:58
  80.9 7.9 %collective-permute-start.18 = (f32[512,128]{1,0:T(8,128)S(1)}, f32[512,128]{1,0:T(8,128)S(1)}, u32[]{:S(2)}, u32[]{:S(2)}) collective-permute-start(f32[512,128]{1,0:T(8,128)S(1)} %add.34), channel_id=1, source_target_pairs={{0,4},{2,6},{4,0},{6,2},{1,5},{3,7},{5,1},{7,3},{8,12},{10,14},{12... | collective-permute-start | bytes 786440 | tf_op jit(solution)/shard_map/ppermute | solution.py:58
  146.9 2.1 %collective-permute-start.20 = (f32[512,128]{1,0:T(8,128)}, f32[512,128]{1,0:T(8,128)S(1)}, u32[]{:S(2)}, u32[]{:S(2)}) collective-permute-start(f32[512,128]{1,0:T(8,128)} %get-tuple-element.52), channel_id=1, source_target_pairs={{0,2},{2,0},{4,6},{6,4},{1,3},{3,1},{5,7},{7,5},{8,10},{10,8},{12,... | collective-permute-start | bytes 786440 | tf_op jit(solution)/shard_map/ppermute | solution.py:58
  147.7 2.7 %collective-permute-start.19 = (f32[512,128]{1,0:T(8,128)S(1)}, f32[512,128]{1,0:T(8,128)S(1)}, u32[]{:S(2)}, u32[]{:S(2)}) collective-permute-start(f32[512,128]{1,0:T(8,128)S(1)} %get-tuple-element.50), channel_id=1, source_target_pairs={{0,2},{2,0},{4,6},{6,4},{1,3},{3,1},{5,7},{7,5},{8,10},{10,8},{12,... | collective-permute-start | bytes 786440 | tf_op jit(solution)/shard_map/ppermute | solution.py:58
  149.1 7.6 %collective-permute-start.21 = (f32[512,128]{1,0:T(8,128)S(1)}, f32[512,128]{1,0:T(8,128)S(1)}, u32[]{:S(2)}, u32[]{:S(2)}) collective-permute-start(f32[512,128]{1,0:T(8,128)S(1)} %add.37), channel_id=1, source_target_pairs={{0,4},{2,6},{4,0},{6,2},{1,5},{3,7},{5,1},{7,3},{8,12},{10,14},{12... | collective-permute-start | bytes 786440 | tf_op jit(solution)/shard_map/ppermute | solution.py:58
  (8 other events, 46.2 us)
Sparse Core Ops, SparseCore 0:
  10.2 112.3 all-gather.1
